TPU v7x, 32 devices: a whole 2x2x4 slice. The times are simulated.
32 devices in a mesh: gx: 8 (over y, x, core), gy: 4 (over z).
Axes of the slice: x: 2, y: 2, z: 4, core: 2. Of those that a mesh axis runs over, the one named last changes fastest.
Arguments:
- state_now: float32 [32, 128, 4096], P(('gx', 'gy')), may hold values from -6 to 6
- state_prev: float32 [32, 128, 4096], P(('gx', 'gy')), may hold values from -6 to 6
- pml_flags: int32 [32], P(('gx', 'gy')), may hold values 0 or 1
- interfaces: int32 [64, 6], P(('gx', 'gy')), may hold values from -16 to 16, as said below
Outputs:
- new_state: float32 [32, 128, 4096], P(('gx', 'gy'))
- face_pressure: float32 [32, 6, 4096], P(('gx', 'gy'))
Inputs may be any that keep to these rules, and one draw needn't show every extreme that they name: `interfaces`: column 0 and column 1 are always 0 (each device holds one box); column 1 names the box of the device one step further along gx and g = column 2 steps across gy; g is -1, 0 or 1 and that device exists whenever column 5 is 1. Columns 3 and 4 are offsets from -16 to 16. Column 5 is 0 exactly on the rows of the last index of gx, which join nothing, and 1 elsewhere.
All inputs are finite; a program needn't handle non-finite values. No bound on the sum of `pml_flags` on one device may be relied on, other than what follows from the above.
Results may differ from a plain program's by a relative error of at most 0.0003.
Values sent between devices are 32-bit elements; how exact they have to be, the bound alone decides.
No kernel may reach another device: no remote copies, remote signals or barrier semaphores. Data moves between devices by JAX's collectives and lax.ppermute only.
A program may use at most 128 MiB of HBM per device.

v0:
```python
import functools
import math

import jax
import jax.numpy as jnp
import ml_dtypes
import numpy as np
from jax import lax
from jax.experimental import pallas as pl
from jax.experimental.pallas import tpu as pltpu
from jax.sharding import PartitionSpec as P

STEPS = 3
OFF = 16
COURANT = 0.4
DAMPING = 0.5
STENCIL = (-490.0, 270.0, -27.0, 2.0)
BLEND = ((1.5, -0.15, 1.0 / 90.0), (-0.15, 1.0 / 90.0, 0.0), (1.0 / 90.0, 0.0, 0.0))
SHIFTS = (-1, 0, 1)
ORDER = (1, 5, 0, 3, 4, 2)
CHUNK = 512
BF16 = ml_dtypes.bfloat16


def cosine_basis(count):
    freqs = np.arange(count)[:, None]
    cells = np.arange(count)[None, :]
    weight = np.where(freqs == 0, np.sqrt(1.0 / count), np.sqrt(2.0 / count))
    return weight * np.cos(math.pi * freqs * (cells + 0.5) / count)


def halves(values):
    high = values.astype(BF16)
    return high, (values - high.astype(np.float64)).astype(BF16)


def twice(block):
    zero = np.zeros_like(block)
    return np.block([[block, zero], [zero, block]])


def banded(count):
    distance = np.abs(np.arange(count)[:, None] - np.arange(count)[None, :])
    weights = np.zeros((count, count))
    for near in (1, 2, 3):
        weights[distance == near] = STENCIL[near]
    return weights


@functools.lru_cache(maxsize=None)
def make_tables(s0, side):
    along = cosine_basis(s0)
    cross = cosine_basis(side)
    wave = (
        ((math.pi * np.arange(s0) / s0) ** 2)[:, None, None]
        + ((math.pi * np.arange(side) / side) ** 2)[None, :, None]
        + ((math.pi * np.arange(side) / side) ** 2)[None, None, :]
    )
    rooted = np.sqrt(wave)
    safe = np.where(wave > 0.0, wave, 1.0)
    gain = np.where(
        wave > 0.0, 4.0 * np.sin(0.5 * COURANT * rooted) ** 2 / safe, COURANT * COURANT
    )
    twice_cosine = 2.0 * np.cos(COURANT * rooted)
    parity = np.arange(s0) % 2
    face = np.zeros((8, s0))
    for r in range(3):
        face[r] = along[:, r] * (parity == 0)
        face[3 + r] = along[:, r] * (parity == 1)
    face_high, face_low = halves(face)
    zero = np.zeros_like(face_low)
    collect = np.block([[face_high, face_high], [face_low, zero]])
    inject = np.concatenate([face_high.T, face_high.T, face_low.T, zero.T], axis=1)
    order = np.concatenate([np.arange(0, side, 2), np.arange(1, side, 2)])
    coupled = []
    for r in range(3):
        for s in range(r, 3):
            parts = [
                np.einsum("k,kab,k->ab", face[3 * o + r], gain, face[3 * o + s])[order] for o in (0, 1)
            ]
            coupled.append(np.concatenate(parts, axis=1))
    forward_one = np.concatenate([*([halves(cross[order])[0]] * 2), halves(cross[order])[1]], axis=1)
    inverse = cross[order].T
    inverse_one = np.concatenate([*([halves(inverse)[0]] * 2), halves(inverse)[1]], axis=1)
    forward_two = np.concatenate([*([halves(twice(cross.T))[0]] * 2), halves(twice(cross.T))[1]], axis=0)
    inverse_two = np.concatenate([*([halves(twice(cross))[0]] * 2), halves(twice(cross))[1]], axis=0)
    rate = DAMPING * ((np.arange(s0) + 0.5) / s0) ** 2
    first = (2.0 + COURANT * COURANT * 3.0 * STENCIL[0] / 180.0) / (1.0 + rate)
    second = -(1.0 - rate) / (1.0 + rate)
    third = COURANT * COURANT / (1.0 + rate)
    rows = [np.broadcast_to(v[:, None], (s0, 128)) for v in (first, second, third / 180.0)]
    ends = np.concatenate([third[:8], third[-8:]])
    down = np.concatenate([banded(s0)] * 2, axis=1).astype(BF16)
    inside = np.concatenate([twice(banded(side))] * 2, axis=0).astype(BF16)
    face_third = np.stack(
        [np.concatenate([np.full(side, third[r]), np.full(side, third[s0 - 1 - r])]) for r in range(3)]
    )
    face_third = np.concatenate([face_third, np.zeros((5, 2 * side))])
    f32 = np.float32
    return {
        "cosine": twice_cosine.reshape(s0, side * side).astype(f32),
        "gain": gain.reshape(s0, side * side).astype(f32),
        "collect": collect,
        "inject": inject,
        "coupled": np.concatenate(coupled, axis=0).astype(f32),
        "forward_one": forward_one,
        "forward_two": forward_two,
        "inverse_one": inverse_one,
        "inverse_two": inverse_two,
        "rows": np.concatenate(rows, axis=0).astype(f32),
        "ends": np.broadcast_to(ends[:, None], (16, 128)).astype(f32),
        "down": down,
        "inside": inside,
        "face_third": face_third.astype(f32),
    }


def pairing(nx, ny, parity, across):
    taken = {}
    for x in range(parity, nx - 1, 2):
        for y in range(ny):
            if 0 <= y + across < ny:
                taken[(x, y)] = (x + 1, y + across)
                taken[(x + 1, y + across)] = (x, y)
    rest = [(x, y) for x in range(nx) for y in range(ny) if (x, y) not in taken]
    while len(rest) > 1:
        x, y = rest.pop(0)
        mate = min(rest, key=lambda d: (abs(d[1] - y) + abs(d[0] // 2 - x // 2), d))
        if parity == 1 and x == 0:
            wrapped = [d for d in rest if d == (nx - 1, y - across)]
            mate = wrapped[0] if wrapped else mate
        rest.remove(mate)
        taken[(x, y)] = mate
        taken[mate] = (x, y)
    return [(x * ny + y, u * ny + v) for (x, y), (u, v) in sorted(taken.items())]


def noted(card):
    bits = card[1][0]
    return card[0][0] > 0, bits & 1 == 1, [bits & (2 << i) != 0 for i in range(len(SHIFTS))]


def position(shape, along, across):
    bits = 1 - along % 2
    for i, g in enumerate(SHIFTS):
        met = (along > 0) & (across - g >= 0) & (across - g < shape[1])
        bits = bits + jnp.where(met, 2 << i, 0)
    return bits


def folded(step, one, two, live):
    return (step + 1) + ((one + OFF) << 2) + ((two + OFF) << 8) + (jnp.where(live, 1, 0) << 14)


def joints(rows_folded, count):
    rows = []
    for n in range(count):
        bits = rows_folded[n, 0]
        rows.append(
            (
                (bits & 3) - 1,
                ((bits >> 2) & 63) - OFF,
                ((bits >> 8) & 63) - OFF,
                (bits >> 14) & 1 == 1,
            )
        )
    return rows


def in_turn(refs):
    return [refs[ORDER.index(i)] for i in range(len(ORDER))]


def left_lanes(shape):
    return lax.broadcasted_iota(jnp.int32, shape, len(shape) - 1) < shape[-1] // 2


def turned(block):
    return pltpu.roll(block, block.shape[-1] // 2, block.ndim - 1)


def two_halves(block):
    high = block.astype(jnp.bfloat16)
    low = (block - high.astype(jnp.float32)).astype(jnp.bfloat16)
    return high, low


def product(a, b):
    return jnp.dot(a, b, preferred_element_type=jnp.float32)


def over_rows(table, block):
    high, low = two_halves(block)
    return product(table, jnp.concatenate([high, low, high], axis=0))


def over_lanes(block, table):
    high, low = two_halves(block)
    return product(jnp.concatenate([high, low, high], axis=1), table)


def beside(planes):
    side = planes.shape[0] // 3
    return jnp.concatenate([planes[r * side : (r + 1) * side] for r in range(3)], axis=1)


def below(planes):
    wide = planes.shape[1] // 3
    return jnp.concatenate([planes[:, r * wide : (r + 1) * wide] for r in range(3)], axis=0)


def sum_difference(block):
    other = turned(block)
    return jnp.where(left_lanes(block.shape), block + other, other - block)


def mirrored_inverse(modes, inverse_one, inverse_two):
    cells = over_rows(inverse_one[...], beside(over_lanes(modes, inverse_two[...])))
    return sum_difference(below(cells))


def mirrored_forward(planes, forward_one, forward_two):
    cells = sum_difference(planes)
    return over_lanes(below(over_rows(forward_one[...], beside(cells))), forward_two[...])


def weave(first, second):
    left = left_lanes(first.shape)
    return jnp.where(left, first, turned(second)), jnp.where(left, turned(first), second)


def blended(planes):
    return [
        sum(BLEND[d][e] * planes[e] for e in range(3) if BLEND[d][e] != 0.0) for d in range(3)
    ]


def emit_payloads(layers, even, listed, outs, pads):
    side = layers.shape[0] // 3
    half = side // 2
    wide = layers.shape[1]
    left = left_lanes((half, wide))
    planes = [layers[r * side : (r + 1) * side] for r in range(3)]
    low = [jnp.where(left, p[:half], turned(p[half:])) for p in planes]
    low = jnp.concatenate(low, axis=0)
    whole = left_lanes((side, wide))
    for r, plane in enumerate(blended(planes)):
        pads[0, r, OFF : OFF + side] = jnp.where(whole, turned(plane), 0.0)
    packed = []
    for _, one, two, _ in listed:
        start = OFF + one
        roll = (wide - two) % wide
        opposite = (wide + side - two) % wide
        parts = []
        for r in range(3):
            top = pltpu.roll(pads[0, r, pl.ds(start, half)], roll, 1)
            bottom = pltpu.roll(pads[0, r, pl.ds(start + half, half)], opposite, 1)
            parts.append(jnp.where(left, top, bottom))
        packed.append(jnp.concatenate(parts, axis=0))
    for i, g in enumerate(SHIFTS):
        force = jnp.zeros_like(low)
        for part, (step, _, _, live) in zip(packed, listed):
            force = force + jnp.where((step == g) & live, part, 0.0)
        outs[i][...] = jnp.where(even, force, low)
        outs[3 + i][...] = jnp.where(even, low, force)


def clear_pads(pads):
    side = pads.shape[2] - 2 * OFF
    blank = jnp.zeros((OFF, pads.shape[3]), jnp.float32)
    for n in range(pads.shape[0]):
        for r in range(3):
            pads[n, r, 0:OFF] = blank
            pads[n, r, OFF + side : 2 * OFF + side] = blank


def take_forces(arrived, even, met, listed, pads):
    wide = arrived[0].shape[1]
    half = arrived[0].shape[0] // 3
    side = 2 * half
    left = left_lanes((half, wide))
    lows = [jnp.where(even, arrived[i][...], arrived[3 + i][...]) for i in range(3)]
    pushes = [jnp.where(even, arrived[3 + i][...], arrived[i][...]) for i in range(3)]
    pushed = jnp.zeros_like(lows[0])
    for i in range(3):
        pushed = pushed + jnp.where(met[i], pushes[i], 0.0)
    high = [None] * 3
    for s, (g, one, two, live) in enumerate(listed):
        chosen = jnp.where(g == 0, lows[1], jnp.where(g < 0, lows[0], lows[2]))
        chosen = jnp.where(live, chosen, 0.0)
        for r in range(3):
            part = chosen[r * half : (r + 1) * half]
            pads[1 + s, r, OFF : OFF + half] = jnp.where(left, part, 0.0)
            pads[1 + s, r, OFF + half : OFF + side] = jnp.where(left, turned(part), 0.0)
        start = OFF - one
        roll = (two + wide + side) % wide
        for r in range(3):
            moved = pltpu.roll(pads[1 + s, r, pl.ds(start, side)], roll, 1)
            high[r] = moved if high[r] is None else high[r] + moved
    high = blended(high)
    planes = []
    for r in range(3):
        part = pushed[r * half : (r + 1) * half]
        lower = jnp.concatenate([part, turned(part)], axis=0)
        planes.append(jnp.where(left_lanes((side, wide)), lower, high[r]))
    return jnp.concatenate(planes, axis=0)


def modal_response(force_modes, coupled):
    side = force_modes.shape[0] // 3
    planes = [force_modes[r * side : (r + 1) * side] for r in range(3)]
    index, n = {}, 0
    for r in range(3):
        for s in range(r, 3):
            index[r, s] = index[s, r] = n
            n += 1
    rows = []
    for r in range(3):
        total = None
        for s in range(3):
            i = index[r, s]
            term = coupled[i * side : (i + 1) * side, :] * planes[s]
            total = term if total is None else total + term
        rows.append(total)
    return jnp.concatenate(rows, axis=0)


def tile_count(ref):
    return ref.shape[1] // 128


def planes_of_modes(gathered, tiles):
    planes = []
    for r in range(3):
        planes += weave(
            gathered[r * tiles : (r + 1) * tiles, :], gathered[(3 + r) * tiles : (4 + r) * tiles, :]
        )
    return jnp.concatenate(planes, axis=0)


def collected(block, collect):
    high, low = two_halves(block)
    both = product(collect[...], jnp.concatenate([high, low], axis=0))
    return both[0:8] + both[8:16]


def scatter_tiles(rows, gathered, column):
    tiles = gathered.shape[0] // 8
    for i in range(rows.shape[1] // 128):
        gathered[pl.ds(column // 128 + i, 8, stride=tiles), :] = rows[:, i * 128 : (i + 1) * 128]


def gather_tiles(gathered, column, width):
    tiles = gathered.shape[0] // 8
    return jnp.concatenate(
        [gathered[pl.ds(column // 128 + i, 8, stride=tiles), :] for i in range(width // 128)], axis=1
    )


def pml_planes(state, gathered, woven):
    s0 = state.shape[0]
    tiles = tile_count(state)
    for start, base in ((0, 0), (s0 - 8, 8 * tiles)):
        for J in range(tiles):
            gathered[pl.ds(base + J, 8, stride=tiles), :] = state[
                start : start + 8, J * 128 : (J + 1) * 128
            ]
    for r in range(3):
        high = (8 + 7 - r) * tiles
        first, second = weave(
            gathered[r * tiles : (r + 1) * tiles, :], gathered[high : high + tiles, :]
        )
        woven[pl.ds(r * 2 * tiles, tiles, stride=2), :] = first
        woven[pl.ds(r * 2 * tiles + 1, tiles, stride=2), :] = second
    return woven[...]


def low_high_rows(planes, woven, tiles):
    woven[...] = planes
    rows = []
    for r in range(3):
        first = woven[pl.ds(r * 2 * tiles, tiles, stride=2), :]
        second = woven[pl.ds(r * 2 * tiles + 1, tiles, stride=2), :]
        rows.append(weave(first, second))
    return rows


def spread_pml_forces(planes, gathered, woven):
    tiles = gathered.shape[0] // 16
    rows = low_high_rows(planes, woven, tiles)
    blank = jnp.zeros((tiles, 128), jnp.float32)
    for s in range(8):
        gathered[s * tiles : (s + 1) * tiles, :] = rows[s][0] if s < 3 else blank
        gathered[(8 + s) * tiles : (9 + s) * tiles, :] = rows[7 - s][1] if s > 4 else blank


def spread_modal_forces(modes, gathered):
    tiles = gathered.shape[0] // 16
    side = modes.shape[0] // 3
    half = side // 2
    blank = jnp.zeros((tiles, 128), jnp.float32)
    for r in range(3):
        plane = modes[r * side : (r + 1) * side]
        even, odd = weave(plane[:half], plane[half:])
        gathered[r * tiles : (r + 1) * tiles, :] = even
        gathered[(3 + r) * tiles : (4 + r) * tiles, :] = odd
    for s in (6, 7):
        gathered[s * tiles : (s + 1) * tiles, :] = blank


def injected(gathered, inject, column, width):
    tiles = gathered.shape[0] // 16
    rows = jnp.concatenate(
        [gathered[pl.ds(column // 128 + i, 8, stride=tiles), :] for i in range(width // 128)], axis=1
    )
    high = rows.astype(jnp.bfloat16).astype(jnp.float32)
    stacked = jnp.concatenate([high, rows - high, high, jnp.zeros_like(rows)], axis=0)
    return product(inject[...], stacked.astype(jnp.bfloat16))


def pml_rows(gathered, column, width, base):
    tiles = gathered.shape[0] // 16
    return jnp.concatenate(
        [
            gathered[pl.ds(base * tiles + column // 128 + i, 8, stride=tiles), :]
            for i in range(width // 128)
        ],
        axis=1,
    )


def wide(rows, width):
    return jnp.concatenate([rows] * (width // 128), axis=1)


def near_sums(state, sums, column, width, down, inside):
    high, low = two_halves(state[:, column : column + width])
    parts = [
        product(
            jnp.concatenate(
                [high[:, i : i + 128], low[:, i : i + 128]], axis=1
            ),
            inside[...],
        )
        for i in range(0, width, 128)
    ]
    total = product(down[...], jnp.concatenate([high, low], axis=0)) + jnp.concatenate(parts, axis=1)
    sums[:, column : column + width] = total


def damped_step(state, before, sums, rows, free, column, width):
    s0, total = state.shape
    first, count = column // 128, width // 128
    left = left_lanes((8, 128))
    blank = jnp.zeros((8, 128), jnp.float32)
    for row in range(0, s0, 8):
        span = slice(row, row + 8)
        own, past, pull = [rows[n * s0 + row : n * s0 + row + 8, :] for n in range(3)]
        near, spun = {}, {}
        for J in range(first - 2, first + count + 2):
            inner = 0 <= J < total // 128
            near[J] = state[span, J * 128 : (J + 1) * 128] if inner else blank
            spun[J] = turned(near[J]) if inner else blank
        half = {
            J: jnp.where(left, spun[J - 1], spun[J]) for J in range(first - 1, first + count + 2)
        }
        for J in range(first, first + count):
            at = slice(J * 128, (J + 1) * 128)
            across = (
                STENCIL[1] * (half[J] + half[J + 1])
                + STENCIL[2] * (near[J - 1] + near[J + 1])
                + STENCIL[3] * (half[J - 1] + half[J + 2])
            )
            free[span, at] = (
                own * near[J] + past * before[span, at] + pull * (sums[span, at] + across)
            )


def copies(pairs, sems, first=0):
    return [
        pltpu.make_async_copy(source, target, sems.at[first + i])
        for i, (source, target) in enumerate(pairs)
    ]


def strips(ref, width=CHUNK):
    return [slice(column, column + width) for column in range(0, ref.shape[-1], width)]


def start_kernel(flags, place, listed, now, before, cosine, *refs):
    sources, outs, folds, refs = refs[:3], in_turn(refs[3:9]), refs[9], refs[10:]
    held, prior, factor, layers, pads, gathered, woven, rows, sems = refs[:9]
    collect, inverse_one, inverse_two = refs[9:]
    total = held.shape[1]
    tiles = total // 128
    spans = strips(held, 2 * CHUNK)
    first = copies([(listed, rows)], sems)
    tables = copies(zip(sources, (collect, inverse_one, inverse_two)), sems, 1)
    moves = copies([(now.at[0, :, p], held.at[:, p]) for p in spans], sems, 4)
    past = copies([(before.at[0], prior)], sems, 4 + len(spans))[0]
    more = copies([(cosine, factor)], sems, 5 + len(spans))[0]
    for m in tables[:1] + moves + tables[1:] + first + [past]:
        m.start()

    @pl.when(flags[0] <= 0)
    def _():
        more.start()

    clear_pads(pads)

    @pl.when(flags[0] > 0)
    def _():
        for m in moves:
            m.wait()
        layers[...] = pml_planes(held, gathered, woven)
        for m in tables:
            m.wait()

    @pl.when(flags[0] <= 0)
    def _():
        tables[0].wait()
        for i, p in enumerate(spans):
            moves[i].wait()
            scatter_tiles(collected(held[:, p], collect), gathered.at[0 : 8 * tiles], p.start)
        for m in tables[1:]:
            m.wait()
        modes = planes_of_modes(gathered, tiles)
        layers[...] = mirrored_inverse(modes, inverse_one, inverse_two)

    first[0].wait()
    entries = []
    for n in range(listed.shape[0]):
        entries.append((rows[n, 2], rows[n, 3], rows[n, 4], rows[n, 5] != 0))
        folds[n : n + 1, :] = jnp.full((1, 128), folded(*entries[n]), jnp.int32)

    _, even, _ = noted((flags, place))
    emit_payloads(layers[...], even, entries, outs, pads)

    past.wait()

    @pl.when(flags[0] <= 0)
    def _():
        more.wait()


def first_kernel(flag, whole, before, cosine, *refs):
    collect, inverse_one, inverse_two, rows, down, inside = refs[:6]
    free, layers, gathered, woven, sums = refs[6:]
    tiles = free.shape[1] // 128
    spans = strips(free, 2 * CHUNK)

    @pl.when(flag[0] > 0)
    def _():
        for p in strips(free):
            near_sums(whole, sums, p.start, CHUNK, down, inside)
        for p in spans:
            damped_step(whole, before, sums, rows, free, p.start, 2 * CHUNK)
        layers[...] = pml_planes(free, gathered, woven)

    @pl.when(flag[0] <= 0)
    def _():
        value = cosine[...] * whole[...] - before[...]
        free[...] = value
        scatter_tiles(collected(value, collect), gathered.at[0 : 8 * tiles], 0)
        layers[...] = mirrored_inverse(planes_of_modes(gathered, tiles), inverse_one, inverse_two)


def free_kernel(flag, forces, _, before, cosine, gain, inject, ends, *refs):
    collect, inverse_one, inverse_two, rows, down, inside, whole = refs[:7]
    free, layers, gathered, woven, sums = refs[7:]
    s0, total = free.shape
    tiles = total // 128

    @pl.when(flag[0] > 0)
    def _():
        spread_pml_forces(forces[...], gathered, woven)
        for p in strips(free):
            for n, at in enumerate((0, s0 - 8)):
                scale = wide(ends[8 * n : 8 * n + 8, :], CHUNK)
                push = pml_rows(gathered, p.start, CHUNK, 8 * n)
                whole[at : at + 8, p] = whole[at : at + 8, p] + scale * push
        for p in strips(free):
            near_sums(whole, sums, p.start, CHUNK, down, inside)
        for p in strips(free, 2 * CHUNK):
            damped_step(whole, before, sums, rows, free, p.start, 2 * CHUNK)
        layers[...] = pml_planes(free, gathered, woven)

    @pl.when(flag[0] <= 0)
    def _():
        spread_modal_forces(forces[...], gathered)
        value = whole[...] + gain[...] * injected(gathered, inject, 0, total)
        whole[...] = value
        value = cosine[...] * value - before[...]
        free[...] = value
        scatter_tiles(collected(value, collect), gathered.at[0 : 8 * tiles], 0)
        layers[...] = mirrored_inverse(planes_of_modes(gathered, tiles), inverse_one, inverse_two)


def pushes(card, folds, arrived, pads):
    clear_pads(pads)
    _, even, met = noted(card)
    return take_forces(arrived, even, met, joints(folds, pads.shape[0] - 1), pads)


def damped_layers(push, layers, face_third):
    side = push.shape[0] // 3
    return jnp.concatenate(
        [
            layers[r * side : (r + 1) * side, :]
            + face_third[r : r + 1, :] * push[r * side : (r + 1) * side]
            for r in range(3)
        ],
        axis=0,
    )


def modal_layers(modes, layers, coupled, inverse_one, inverse_two):
    return layers[...] + mirrored_inverse(modal_response(modes, coupled), inverse_one, inverse_two)


def force_kernel(*refs):
    card, folds, refs = refs[:2], refs[2], refs[3:]
    arrived, layers, tables = in_turn(refs[:6]), refs[6], refs[7:13]
    forces, outs, (next_layers, pads) = refs[13], in_turn(refs[14:20]), refs[20:]
    coupled, forward_one, forward_two, inverse_one, inverse_two, face_third = tables
    damped, even, _ = noted(card)
    push = pushes(card, folds, arrived, pads)

    @pl.when(damped)
    def _():
        forces[...] = push
        next_layers[...] = damped_layers(push, layers, face_third)

    @pl.when(jnp.logical_not(damped))
    def _():
        modes = mirrored_forward(push, forward_one, forward_two)
        forces[...] = modes
        next_layers[...] = modal_layers(modes, layers, coupled, inverse_one, inverse_two)

    emit_payloads(next_layers[...], even, joints(folds, pads.shape[0] - 1), outs, pads)


def last_kernel(*refs):
    card, folds, refs = refs[:2], refs[2], refs[3:]
    arrived, layers, tables = in_turn(refs[:6]), refs[6], refs[7:13]
    free, gain, inject, rims = refs[13:17]
    state, faces, pads, gathered, shown, woven, held, sems = refs[17:]
    coupled, forward_one, forward_two, inverse_one, inverse_two, face_third = tables
    damped, _, _ = noted(card)
    s0, total = free.shape
    tiles = total // 128
    middle = slice(8, s0 - 8)
    ends = (0, s0 - 8)
    inner = copies([(free.at[middle], state.at[0, middle])], sems)
    outer = copies([(held.at[at : at + 8], state.at[0, at : at + 8]) for at in ends], sems, 1)
    broad = strips(free, 2 * CHUNK)
    moves = copies([(held.at[:, p], state.at[0, :, p]) for p in broad], sems)

    def show(values):
        for r, pair in enumerate(low_high_rows(values, woven, tiles)):
            for i, rows in enumerate(pair):
                shown[(3 * i + r) * tiles : (3 * i + r + 1) * tiles, :] = rows

    @pl.when(damped)
    def _():
        inner[0].start()

    push = pushes(card, folds, arrived, pads)

    @pl.when(damped)
    def _():
        spread_pml_forces(push, gathered, woven)
        for p in strips(free):
            for n, at in enumerate(ends):
                scale = wide(rims[8 * n : 8 * n + 8, :], CHUNK)
                moved = pml_rows(gathered, p.start, CHUNK, 8 * n)
                held[at : at + 8, p] = free[at : at + 8, p] + scale * moved
        for m in outer:
            m.start()
        show(damped_layers(push, layers, face_third))

    @pl.when(jnp.logical_not(damped))
    def _():
        modes = mirrored_forward(push, forward_one, forward_two)
        spread_modal_forces(modes, gathered)
        show(modal_layers(modes, layers, coupled, inverse_one, inverse_two))
        for m, p in zip(moves, broad):
            moved = injected(gathered, inject, p.start, 2 * CHUNK)
            held[:, p] = free[:, p] + gain[:, p] * moved
            m.start()

    last = pltpu.make_async_copy(shown, faces, sems.at[len(broad)])
    last.start()

    @pl.when(damped)
    def _():
        for m in inner + outer:
            m.wait()

    @pl.when(jnp.logical_not(damped))
    def _():
        for m in moves:
            m.wait()

    last.wait()


SCALAR = pl.BlockSpec(memory_space=pltpu.SMEM)
BLOCK = pl.BlockSpec(memory_space=pltpu.VMEM)
FAR = pl.BlockSpec(memory_space=pltpu.HBM)


def run(body, blocks, outs, scratch, near=(), far=(), far_outs=(), aliases=None, flops=0):
    moved = sum(b.size * b.dtype.itemsize for b in blocks)
    blocks = [
        pltpu.with_memory_space_constraint(b, pltpu.HBM) if i in far else b
        for i, b in enumerate(blocks)
    ]
    spots = {**dict.fromkeys(far, FAR), **dict.fromkeys(near, SCALAR)}
    return pl.pallas_call(
        body,
        out_shape=[
            jax.ShapeDtypeStruct(s, jnp.float32) if isinstance(s, tuple) else s for s in outs
        ],
        in_specs=[spots.get(i, BLOCK) for i in range(len(blocks))],
        out_specs=[
            FAR if i in far_outs else BLOCK
            for i, s in enumerate(outs)
        ],
        scratch_shapes=[
            pltpu.VMEM(s, jnp.float32) if isinstance(s, tuple) else s for s in scratch
        ],
        input_output_aliases=aliases or {},
        compiler_params=pltpu.CompilerParams(vmem_limit_bytes=32 * 1024 * 1024),
        cost_estimate=pl.CostEstimate(flops=flops, bytes_accessed=moved, transcendentals=0),
    )(*blocks)


def local(nx, ny, state_now, state_prev, pml_flags, interfaces):
    _, s0, cross = state_now.shape
    side = math.isqrt(cross)
    t = {k: jnp.asarray(v) for k, v in make_tables(s0, side).items()}
    tiles = cross // 128
    planes = (3 * side, 128)
    packed = (3 * side // 2, 128)
    pads = (1 + interfaces.shape[0], 3, side + 2 * OFF, 128)
    gathered = (16 * tiles, 128)
    full = (s0, cross)
    count = cross // CHUNK
    place = position((nx, ny), lax.axis_index("gx"), lax.axis_index("gy")).reshape(1)
    card = (pml_flags, place)
    routes = [pairing(nx, ny, parity, g) for parity in (0, 1) for g in SHIFTS]

    def exchange(payloads):
        return [lax.ppermute(payloads[k], ("gx", "gy"), routes[i]) for k, i in enumerate(ORDER)]

    *payloads, folds, now, prior, cosine = run(
        start_kernel,
        (
            *(pml_flags, place, interfaces, state_now, state_prev, t["cosine"]),
            *(t["collect"], t["inverse_one"], t["inverse_two"]),
        ),
        [packed] * 6 + [jax.ShapeDtypeStruct((8, 128), jnp.int32)] + [full] * 3,
        [
            *(planes, pads, gathered, planes),
            pltpu.SMEM(interfaces.shape, jnp.int32),
            pltpu.SemaphoreType.DMA((6 + count,)),
            *(pltpu.VMEM(t[k].shape, t[k].dtype) for k in ("collect", "inverse_one", "inverse_two")),
        ],
        near=(0, 1),
        far=range(2, 9),
    )
    names = ("coupled", "forward_one", "forward_two", "inverse_one", "inverse_two", "face_third")
    tables = [t[k] for k in names]
    shared = [t[k] for k in ("collect", "inverse_one", "inverse_two", "rows", "down", "inside")]
    for step in range(STEPS):
        arrived = exchange(payloads)
        if step == 0:
            free, layers = run(
                first_kernel,
                (pml_flags, now, prior, cosine, *shared),
                [full, planes],
                [gathered, planes, full],
                near=(0,),
                flops=10**9,
            )
        else:
            now, free, layers = run(
                free_kernel,
                (pml_flags, forces, free, now, cosine, t["gain"], t["inject"], t["ends"], *shared),
                [full, full, planes],
                [gathered, planes, full],
                near=(0,),
                aliases={2: 0},
                flops=10**9,
            )
        if step < STEPS - 1:
            forces, *payloads = run(
                force_kernel,
                (*card, folds, *arrived, layers, *tables),
                [planes] + [packed] * 6,
                [planes, pads],
                near=(0, 1),
            )
    state, faces = run(
        last_kernel,
        (*card, folds, *arrived, layers, *tables, free, t["gain"], t["inject"], t["ends"]),
        [(1, s0, cross), (6 * tiles, 128)],
        [
            *(pads, gathered, (6 * tiles, 128), planes, full),
            pltpu.SemaphoreType.DMA((3 + count,)),
        ],
        near=(0, 1),
        far_outs=(0, 1),
    )
    return state, faces.reshape(1, 6, cross)


def solution(mesh):
    placed = (
        P(("gx", "gy"), None, None),
        P(("gx", "gy"), None, None),
        P(("gx", "gy")),
        P(("gx", "gy"), None),
    )
    return jax.shard_map(
        functools.partial(local, mesh.shape["gx"], mesh.shape["gy"]),
        mesh=mesh,
        in_specs=placed,
        out_specs=(P(("gx", "gy"), None, None), P(("gx", "gy"), None, None)),
        check_vma=False,
    )
```

profile of v0, /device:TPU:0, one launch (start us, length us, event | category | flops | bytes accessed | tf_op | source)
XLA Modules:
  0.0 39.7 jit_solution(54617627423029643)
XLA Ops:
  1.3 0.0 copy-start.1
  1.3 0.0 copy-start.3
  1.3 0.0 copy-start.4
  1.3 0.0 copy-start.6
  1.4 0.0 copy-start.7
  1.4 0.0 copy-start.10
  1.4 3.2 %shard_map.185 = (f32[96,128]{1,0:T(8,128)S(1)}, f32[96,128]{1,0:T(8,128)S(1)}, f32[96,128]{1,0:T(8,128)S(1)}, f32[96,128]{1,0:T(8,128)S(1)}, f32[96,128]{1,0:T(...) custom-call(s32[1]{0:T(128)S(6)} %copy.26.flags.flag.refs_0_, ...), custom_call_target="tpu_custom_call" | custom-call | bytes 6422584 | tf_op jit(solution)/shard_map/pallas_call | solution.py:720
  4.5 0.1 collective-permute-start
  4.6 3.1 %collective-permute-start.1 = (f32[96,128]{1,0:T(8,128)S(1)}, f32[96,128]{1,0:T(8,128)S(1)}, u32[]{:S(2)}, u32[]{:S(2)}) collective-permute-start(f32[96,128]{1,0:T(8,128)S(1)} %get-tuple-element.37), channel_id=1, source_target_pairs={{0,1},{1,0},{2,29},{3,30},{4,9},{5,10},{6,11},{7,15},{8,16},{9,4},... | collective-permute-start | bytes 147464 | tf_op jit(solution)/shard_map/ppermute | solution.py:755
  7.7 0.8 %collective-permute-start.2 = (f32[96,128]{1,0:T(8,128)S(1)}, f32[96,128]{1,0:T(8,128)S(1)}, u32[]{:S(2)}, u32[]{:S(2)}) collective-permute-start(f32[96,128]{1,0:T(8,128)S(1)} %get-tuple-element.38), channel_id=1, source_target_pairs={{0,8},{1,4},{2,5},{3,6},{4,1},{5,2},{6,3},{7,15},{8,0},{9,12},{10,... | collective-permute-start | bytes 147464 | tf_op jit(solution)/shard_map/ppermute | solution.py:755
  8.5 2.9 %collective-permute-start.3 = (f32[96,128]{1,0:T(8,128)S(1)}, f32[96,128]{1,0:T(8,128)S(1)}, u32[]{:S(2)}, u32[]{:S(2)}) collective-permute-start(f32[96,128]{1,0:T(8,128)S(1)} %get-tuple-element.39), channel_id=1, source_target_pairs={{0,29},{1,30},{2,31},{3,11},{4,12},{5,8},{6,9},{7,10},{8,5},{9,6},... | collective-permute-start | bytes 147464 | tf_op jit(solution)/shard_map/ppermute | solution.py:755
  11.4 0.1 collective-permute-start.4
  11.5 2.0 %collective-permute-start.5 = (f32[96,128]{1,0:T(8,128)S(1)}, f32[96,128]{1,0:T(8,128)S(1)}, u32[]{:S(2)}, u32[]{:S(2)}) collective-permute-start(f32[96,128]{1,0:T(8,128)S(1)} %get-tuple-element.41), channel_id=1, source_target_pairs={{0,5},{1,6},{2,7},{3,11},{4,12},{5,0},{6,1},{7,2},{8,13},{9,14},{1... | collective-permute-start | bytes 147464 | tf_op jit(solution)/shard_map/ppermute | solution.py:755
  13.6 0.0 copy-start.2
  13.6 0.0 copy-start.5
  13.6 0.0 copy-start.9
  13.6 0.0 copy-start.12
  13.6 0.0 copy-start
  13.6 0.0 copy-start.8
  13.7 0.0 copy-start.11
  13.7 1.2 %shard_map.186 = (f32[128,4096]{1,0:T(8,128)S(1)}, f32[192,128]{1,0:T(8,128)S(1)}) custom-call(s32[1]{0:T(128)S(6)} %copy.26.flags.flag.refs_0_, f32[128,4096]{1,0:T(8,128)S(1)} %get-tuple-element.42.whole.before, f32[128,4096]{1,0:T(8,128)S(1)} %get-tuple-element.43.before, f32[128,4096]{1,0:T(8,128)S(1)} %get-tuple-element.44.cosine, ...), custom_call_target="tpu_custom_call" | custom-call | flops 1000000000 | bytes 6750212 | tf_op jit(solution)/shard_map/pallas_call | solution.py:720
  14.9 0.0 collective-permute-done.1.refs_4_
  14.9 0.0 collective-permute-done.3.refs_6_
  14.9 0.9 %collective-permute-done.4.refs_7_ = f32[96,128]{1,0:T(8,128)S(1)} collective-permute-done((f32[96,128]{1,0:T(8,128)S(1)}, f32[96,128]{1,0:T(8,128)S(1)}, u32[]{:S(2)}, u32[]{:S(2)}) %collective-permute-start.4) | collective-permute-done | bytes 49184 | tf_op jit(solution)/shard_map/ppermute | solution.py:755
  15.8 0.0 collective-permute-done.5.refs_8_
  15.8 1.3 %shard_map.187 = (f32[192,128]{1,0:T(8,128)S(1)}, f32[96,128]{1,0:T(8,128)S(1)}, f32[96,128]{1,0:T(8,128)S(1)}, f32[96,128]{1,0:T(8,128)S(1)}, f32[96,128]{1,0:T...) custom-call(s32[1]{0:T(128)S(6)} %copy.26.flags.flag.refs_0_, s32[1]{0:T(128)} %bitcast.place.refs_1_, ...), custom_call_target="tpu_custom_call" | custom-call | bytes 843784 | tf_op jit(solution)/shard_map/pallas_call | solution.py:720
  17.1 0.1 collective-permute-start.6
  17.2 1.7 %collective-permute-start.7 = (f32[96,128]{1,0:T(8,128)S(1)}, f32[96,128]{1,0:T(8,128)S(1)}, u32[]{:S(2)}, u32[]{:S(2)}) collective-permute-start(f32[96,128]{1,0:T(8,128)S(1)} %get-tuple-element.47), channel_id=1, source_target_pairs={{0,1},{1,0},{2,29},{3,30},{4,9},{5,10},{6,11},{7,15},{8,16},{9,4},... | collective-permute-start | bytes 147464 | tf_op jit(solution)/shard_map/ppermute | solution.py:755
  18.8 0.5 %collective-permute-start.8 = (f32[96,128]{1,0:T(8,128)S(1)}, f32[96,128]{1,0:T(8,128)S(1)}, u32[]{:S(2)}, u32[]{:S(2)}) collective-permute-start(f32[96,128]{1,0:T(8,128)S(1)} %get-tuple-element.48), channel_id=1, source_target_pairs={{0,8},{1,4},{2,5},{3,6},{4,1},{5,2},{6,3},{7,15},{8,0},{9,12},{10,... | collective-permute-start | bytes 147464 | tf_op jit(solution)/shard_map/ppermute | solution.py:755
  19.3 3.1 %collective-permute-start.9 = (f32[96,128]{1,0:T(8,128)S(1)}, f32[96,128]{1,0:T(8,128)S(1)}, u32[]{:S(2)}, u32[]{:S(2)}) collective-permute-start(f32[96,128]{1,0:T(8,128)S(1)} %get-tuple-element.49), channel_id=1, source_target_pairs={{0,29},{1,30},{2,31},{3,11},{4,12},{5,8},{6,9},{7,10},{8,5},{9,6},... | collective-permute-start | bytes 147464 | tf_op jit(solution)/shard_map/ppermute | solution.py:755
  22.4 0.0 collective-permute-start.10
  22.4 0.0 collective-permute-done.6.refs_3_
  22.4 1.9 %collective-permute-start.11 = (f32[96,128]{1,0:T(8,128)S(1)}, f32[96,128]{1,0:T(8,128)S(1)}, u32[]{:S(2)}, u32[]{:S(2)}) collective-permute-start(f32[96,128]{1,0:T(8,128)S(1)} %get-tuple-element.51), channel_id=1, source_target_pairs={{0,5},{1,6},{2,7},{3,11},{4,12},{5,0},{6,1},{7,2},{8,13},{9,14},{1... | collective-permute-start | bytes 147464 | tf_op jit(solution)/shard_map/ppermute | solution.py:755
  24.2 1.7 %shard_map.188 = (f32[128,4096]{1,0:T(8,128)S(1)}, f32[128,4096]{1,0:T(8,128)S(1)}, f32[192,128]{1,0:T(8,128)S(1)}) custom-call(s32[1]{0:T(128)S(6)} %copy.26.flags.flag.refs_0_, f32[192,128]{1,0:T(8,128)S(1)} %get-tuple-element.52.forces, f32[128,4096]{1,0:T(8,128)S(1)} %get-tuple-element.53._, ...), custom_call_target="tpu_custom_call", output_to_operand_aliasing={{0}: (2, {})} | custom-call | flops 1000000000 | bytes 8962052 | tf_op jit(solution)/shard_map/pallas_call | solution.py:720
  25.9 0.0 collective-permute-done.7.refs_4_
  26.0 0.0 collective-permute-done.9.refs_6_
  26.0 0.8 %collective-permute-done.10.refs_7_ = f32[96,128]{1,0:T(8,128)S(1)} collective-permute-done((f32[96,128]{1,0:T(8,128)S(1)}, f32[96,128]{1,0:T(8,128)S(1)}, u32[]{:S(2)}, u32[]{:S(2)}) %collective-permute-start.10) | collective-permute-done | bytes 49184 | tf_op jit(solution)/shard_map/ppermute | solution.py:755
  26.8 0.0 collective-permute-done.11.refs_8_
  26.8 1.3 %shard_map.189 = (f32[192,128]{1,0:T(8,128)S(1)}, f32[96,128]{1,0:T(8,128)S(1)}, f32[96,128]{1,0:T(8,128)S(1)}, f32[96,128]{1,0:T(8,128)S(1)}, f32[96,128]{1,0:T...) custom-call(s32[1]{0:T(128)S(6)} %copy.26.flags.flag.refs_0_, s32[1]{0:T(128)} %bitcast.place.refs_1_, ...), custom_call_target="tpu_custom_call" | custom-call | bytes 843784 | tf_op jit(solution)/shard_map/pallas_call | solution.py:720
  28.1 0.1 collective-permute-start.12
  28.2 1.3 %collective-permute-start.13 = (f32[96,128]{1,0:T(8,128)S(1)}, f32[96,128]{1,0:T(8,128)S(1)}, u32[]{:S(2)}, u32[]{:S(2)}) collective-permute-start(f32[96,128]{1,0:T(8,128)S(1)} %get-tuple-element.56), channel_id=1, source_target_pairs={{0,1},{1,0},{2,29},{3,30},{4,9},{5,10},{6,11},{7,15},{8,16},{9,4},... | collective-permute-start | bytes 147464 | tf_op jit(solution)/shard_map/ppermute | solution.py:755
  29.5 1.0 %collective-permute-start.14 = (f32[96,128]{1,0:T(8,128)S(1)}, f32[96,128]{1,0:T(8,128)S(1)}, u32[]{:S(2)}, u32[]{:S(2)}) collective-permute-start(f32[96,128]{1,0:T(8,128)S(1)} %get-tuple-element.57), channel_id=1, source_target_pairs={{0,8},{1,4},{2,5},{3,6},{4,1},{5,2},{6,3},{7,15},{8,0},{9,12},{10,... | collective-permute-start | bytes 147464 | tf_op jit(solution)/shard_map/ppermute | solution.py:755
  30.4 2.2 %collective-permute-start.15 = (f32[96,128]{1,0:T(8,128)S(1)}, f32[96,128]{1,0:T(8,128)S(1)}, u32[]{:S(2)}, u32[]{:S(2)}) collective-permute-start(f32[96,128]{1,0:T(8,128)S(1)} %get-tuple-element.58), channel_id=1, source_target_pairs={{0,29},{1,30},{2,31},{3,11},{4,12},{5,8},{6,9},{7,10},{8,5},{9,6},... | collective-permute-start | bytes 147464 | tf_op jit(solution)/shard_map/ppermute | solution.py:755
  32.7 1.1 %collective-permute-start.17 = (f32[96,128]{1,0:T(8,128)S(1)}, f32[96,128]{1,0:T(8,128)S(1)}, u32[]{:S(2)}, u32[]{:S(2)}) collective-permute-start(f32[96,128]{1,0:T(8,128)S(1)} %get-tuple-element.60), channel_id=1, source_target_pairs={{0,5},{1,6},{2,7},{3,11},{4,12},{5,0},{6,1},{7,2},{8,13},{9,14},{1... | collective-permute-start | bytes 147464 | tf_op jit(solution)/shard_map/ppermute | solution.py:755
  33.7 1.7 %shard_map.190 = (f32[128,4096]{1,0:T(8,128)S(1)}, f32[128,4096]{1,0:T(8,128)S(1)}, f32[192,128]{1,0:T(8,128)S(1)}) custom-call(s32[1]{0:T(128)S(6)} %copy.26.flags.flag.refs_0_, f32[192,128]{1,0:T(8,128)S(1)} %get-tuple-element.61.forces, f32[128,4096]{1,0:T(8,128)S(1)} %get-tuple-element.62._, ...), custom_call_target="tpu_custom_call", output_to_operand_aliasing={{0}: (2, {})} | custom-call | flops 1000000000 | bytes 8962052 | tf_op jit(solution)/shard_map/pallas_call | solution.py:720
  35.5 0.3 collective-permute-done.15.refs_6_
  35.8 1.3 %collective-permute-done.16.refs_7_ = f32[96,128]{1,0:T(8,128)S(1)} collective-permute-done((f32[96,128]{1,0:T(8,128)S(1)}, f32[96,128]{1,0:T(8,128)S(1)}, u32[]{:S(2)}, u32[]{:S(2)}) %collective-permute-start.16) | collective-permute-done | bytes 49184 | tf_op jit(solution)/shard_map/ppermute | solution.py:755
  37.1 2.5 %shard_map.191 = (f32[1,128,4096]{2,1,0:T(8,128)}, f32[192,128]{1,0:T(8,128)}) custom-call(s32[1]{0:T(128)S(6)} %copy.26.flags.flag.refs_0_, s32[1]{0:T(128)} %bitcast.place.refs_1_, s32[8,128]{1,0:T(8,128)S(1)} %get-tuple-element.35.refs_2_, f32[96,128]{1,0:T(8,128)S(1)} %collective-permute-done.12.refs_3_, f32[96,128]{1,0:T(8,128)S(1)} %collective-permute-done.13.refs_4_, ...), custom_call_target="tpu_custom_call" | custom-call | bytes 5054472 | tf_op jit(solution)/shard_map/pallas_call | solution.py:720
  (21 shorter events, 0.0 us)
Async XLA Ops:
  1.3 12.2 %copy-start.1 = (bf16[384,128]{1,0:T(8,128)(2,1)S(1)}, bf16[384,128]{1,0:T(8,128)(2,1)}, u32[]{:S(2)}) copy-start(bf16[384,128]{1,0:T(8,128)(2,1)} %constant.68.clone.refs_2_.refs_14_) | copy-start | bytes 294916
  1.3 12.2 %copy-start.3 = (f32[384,128]{1,0:T(8,128)S(1)}, f32[384,128]{1,0:T(8,128)}, u32[]{:S(2)}) copy-start(f32[384,128]{1,0:T(8,128)} %constant.69.clone.refs_3_) | copy-start | bytes 589828
  1.3 12.2 %copy-start.4 = (bf16[64,192]{1,0:T(8,128)(2,1)S(1)}, bf16[64,192]{1,0:T(8,128)(2,1)}, u32[]{:S(2)}) copy-start(bf16[64,192]{1,0:T(8,128)(2,1)} %constant.67.clone.refs_1_.refs_13_) | copy-start | bytes 73732
  1.3 12.2 %copy-start.6 = (bf16[128,256]{1,0:T(8,128)(2,1)S(1)}, bf16[128,256]{1,0:T(8,128)(2,1)}, u32[]{:S(2)}) copy-start(bf16[128,256]{1,0:T(8,128)(2,1)} %constant.71.clone.refs_4_) | copy-start | bytes 196612
  1.4 12.2 %copy-start.7 = (bf16[256,128]{1,0:T(8,128)(2,1)S(1)}, bf16[256,128]{1,0:T(8,128)(2,1)}, u32[]{:S(2)}) copy-start(bf16[256,128]{1,0:T(8,128)(2,1)} %constant.72.clone.refs_5_) | copy-start | bytes 196612
  1.4 12.2 %copy-start.10 = (bf16[16,256]{1,0:T(8,128)(2,1)S(1)}, bf16[16,256]{1,0:T(8,128)(2,1)}, u32[]{:S(2)}) copy-start(bf16[16,256]{1,0:T(8,128)(2,1)} %constant.62.clone.refs_0_) | copy-start | bytes 24580
  4.5 7.0 %collective-permute-start = (f32[96,128]{1,0:T(8,128)S(1)}, f32[96,128]{1,0:T(8,128)S(1)}, u32[]{:S(2)}, u32[]{:S(2)}) collective-permute-start(f32[96,128]{1,0:T(8,128)S(1)} %get-tuple-element.36), channel_id=1, source_target_pairs={{0,4},{1,5},{2,6},{3,7},{4,0},{5,1},{6,2},{7,3},{8,12},{9,13},{10,... | collective-permute-start | bytes 147464 | tf_op jit(solution)/shard_map/ppermute | solution.py:755
  4.6 10.3 %collective-permute-start.1 = (f32[96,128]{1,0:T(8,128)S(1)}, f32[96,128]{1,0:T(8,128)S(1)}, u32[]{:S(2)}, u32[]{:S(2)}) collective-permute-start(f32[96,128]{1,0:T(8,128)S(1)} %get-tuple-element.37), channel_id=1, source_target_pairs={{0,1},{1,0},{2,29},{3,30},{4,9},{5,10},{6,11},{7,15},{8,16},{9,4},... | collective-permute-start | bytes 147464 | tf_op jit(solution)/shard_map/ppermute | solution.py:755
  7.7 7.2 %collective-permute-start.2 = (f32[96,128]{1,0:T(8,128)S(1)}, f32[96,128]{1,0:T(8,128)S(1)}, u32[]{:S(2)}, u32[]{:S(2)}) collective-permute-start(f32[96,128]{1,0:T(8,128)S(1)} %get-tuple-element.38), channel_id=1, source_target_pairs={{0,8},{1,4},{2,5},{3,6},{4,1},{5,2},{6,3},{7,15},{8,0},{9,12},{10,... | collective-permute-start | bytes 147464 | tf_op jit(solution)/shard_map/ppermute | solution.py:755
  8.5 6.4 %collective-permute-start.3 = (f32[96,128]{1,0:T(8,128)S(1)}, f32[96,128]{1,0:T(8,128)S(1)}, u32[]{:S(2)}, u32[]{:S(2)}) collective-permute-start(f32[96,128]{1,0:T(8,128)S(1)} %get-tuple-element.39), channel_id=1, source_target_pairs={{0,29},{1,30},{2,31},{3,11},{4,12},{5,8},{6,9},{7,10},{8,5},{9,6},... | collective-permute-start | bytes 147464 | tf_op jit(solution)/shard_map/ppermute | solution.py:755
  11.4 4.4 %collective-permute-start.4 = (f32[96,128]{1,0:T(8,128)S(1)}, f32[96,128]{1,0:T(8,128)S(1)}, u32[]{:S(2)}, u32[]{:S(2)}) collective-permute-start(f32[96,128]{1,0:T(8,128)S(1)} %get-tuple-element.40), channel_id=1, source_target_pairs={{0,28},{1,29},{2,30},{3,31},{4,8},{5,9},{6,10},{7,11},{8,4},{9,5},... | collective-permute-start | bytes 147464 | tf_op jit(solution)/shard_map/ppermute | solution.py:755
  11.5 4.3 %collective-permute-start.5 = (f32[96,128]{1,0:T(8,128)S(1)}, f32[96,128]{1,0:T(8,128)S(1)}, u32[]{:S(2)}, u32[]{:S(2)}) collective-permute-start(f32[96,128]{1,0:T(8,128)S(1)} %get-tuple-element.41), channel_id=1, source_target_pairs={{0,5},{1,6},{2,7},{3,11},{4,12},{5,0},{6,1},{7,2},{8,13},{9,14},{1... | collective-permute-start | bytes 147464 | tf_op jit(solution)/shard_map/ppermute | solution.py:755
  13.6 2.2 %copy-start.2 = (f32[384,128]{1,0:T(8,128)S(1)}, f32[384,128]{1,0:T(8,128)}, u32[]{:S(2)}) copy-start(f32[384,128]{1,0:T(8,128)} %constant.64.clone.refs_10_) | copy-start | bytes 589828
  13.6 2.2 %copy-start.5 = (bf16[384,128]{1,0:T(8,128)(2,1)S(1)}, bf16[384,128]{1,0:T(8,128)(2,1)}, u32[]{:S(2)}) copy-start(bf16[384,128]{1,0:T(8,128)(2,1)} %constant.66.clone.refs_12_) | copy-start | bytes 294916
  13.6 2.2 %copy-start.9 = (bf16[64,192]{1,0:T(8,128)(2,1)S(1)}, bf16[64,192]{1,0:T(8,128)(2,1)}, u32[]{:S(2)}) copy-start(bf16[64,192]{1,0:T(8,128)(2,1)} %constant.65.clone.refs_11_) | copy-start | bytes 73732
  13.6 2.2 %copy-start.12 = (f32[8,128]{1,0:T(8,128)S(1)}, f32[8,128]{1,0:T(8,128)}, u32[]{:S(2)}) copy-start(f32[8,128]{1,0:T(8,128)} %constant.73.clone.refs_15_) | copy-start | bytes 12292
  13.6 10.6 %copy-start = (f32[128,4096]{1,0:T(8,128)S(1)}, f32[128,4096]{1,0:T(8,128)}, u32[]{:S(2)}) copy-start(f32[128,4096]{1,0:T(8,128)} %constant.61.clone.gain.refs_17_) | copy-start | bytes 6291460
  13.6 10.6 %copy-start.8 = (bf16[128,32]{1,0:T(8,128)(2,1)S(1)}, bf16[128,32]{1,0:T(8,128)(2,1)}, u32[]{:S(2)}) copy-start(bf16[128,32]{1,0:T(8,128)(2,1)} %constant.63.clone.inject.refs_18_) | copy-start | bytes 24580
  13.7 10.6 %copy-start.11 = (f32[16,128]{1,0:T(8,128)S(1)}, f32[16,128]{1,0:T(8,128)}, u32[]{:S(2)}) copy-start(f32[16,128]{1,0:T(8,128)} %constant.70.clone.ends.refs_19_) | copy-start | bytes 24580
  17.1 5.3 %collective-permute-start.6 = (f32[96,128]{1,0:T(8,128)S(1)}, f32[96,128]{1,0:T(8,128)S(1)}, u32[]{:S(2)}, u32[]{:S(2)}) collective-permute-start(f32[96,128]{1,0:T(8,128)S(1)} %get-tuple-element.46), channel_id=1, source_target_pairs={{0,4},{1,5},{2,6},{3,7},{4,0},{5,1},{6,2},{7,3},{8,12},{9,13},{10,... | collective-permute-start | bytes 147464 | tf_op jit(solution)/shard_map/ppermute | solution.py:755
  17.2 8.8 %collective-permute-start.7 = (f32[96,128]{1,0:T(8,128)S(1)}, f32[96,128]{1,0:T(8,128)S(1)}, u32[]{:S(2)}, u32[]{:S(2)}) collective-permute-start(f32[96,128]{1,0:T(8,128)S(1)} %get-tuple-element.47), channel_id=1, source_target_pairs={{0,1},{1,0},{2,29},{3,30},{4,9},{5,10},{6,11},{7,15},{8,16},{9,4},... | collective-permute-start | bytes 147464 | tf_op jit(solution)/shard_map/ppermute | solution.py:755
  18.8 7.1 %collective-permute-start.8 = (f32[96,128]{1,0:T(8,128)S(1)}, f32[96,128]{1,0:T(8,128)S(1)}, u32[]{:S(2)}, u32[]{:S(2)}) collective-permute-start(f32[96,128]{1,0:T(8,128)S(1)} %get-tuple-element.48), channel_id=1, source_target_pairs={{0,8},{1,4},{2,5},{3,6},{4,1},{5,2},{6,3},{7,15},{8,0},{9,12},{10,... | collective-permute-start | bytes 147464 | tf_op jit(solution)/shard_map/ppermute | solution.py:755
  19.3 6.7 %collective-permute-start.9 = (f32[96,128]{1,0:T(8,128)S(1)}, f32[96,128]{1,0:T(8,128)S(1)}, u32[]{:S(2)}, u32[]{:S(2)}) collective-permute-start(f32[96,128]{1,0:T(8,128)S(1)} %get-tuple-element.49), channel_id=1, source_target_pairs={{0,29},{1,30},{2,31},{3,11},{4,12},{5,8},{6,9},{7,10},{8,5},{9,6},... | collective-permute-start | bytes 147464 | tf_op jit(solution)/shard_map/ppermute | solution.py:755
  22.4 4.4 %collective-permute-start.10 = (f32[96,128]{1,0:T(8,128)S(1)}, f32[96,128]{1,0:T(8,128)S(1)}, u32[]{:S(2)}, u32[]{:S(2)}) collective-permute-start(f32[96,128]{1,0:T(8,128)S(1)} %get-tuple-element.50), channel_id=1, source_target_pairs={{0,28},{1,29},{2,30},{3,31},{4,8},{5,9},{6,10},{7,11},{8,4},{9,5},... | collective-permute-start | bytes 147464 | tf_op jit(solution)/shard_map/ppermute | solution.py:755
  22.4 4.4 %collective-permute-start.11 = (f32[96,128]{1,0:T(8,128)S(1)}, f32[96,128]{1,0:T(8,128)S(1)}, u32[]{:S(2)}, u32[]{:S(2)}) collective-permute-start(f32[96,128]{1,0:T(8,128)S(1)} %get-tuple-element.51), channel_id=1, source_target_pairs={{0,5},{1,6},{2,7},{3,11},{4,12},{5,0},{6,1},{7,2},{8,13},{9,14},{1... | collective-permute-start | bytes 147464 | tf_op jit(solution)/shard_map/ppermute | solution.py:755
  28.1 4.6 %collective-permute-start.12 = (f32[96,128]{1,0:T(8,128)S(1)}, f32[96,128]{1,0:T(8,128)S(1)}, u32[]{:S(2)}, u32[]{:S(2)}) collective-permute-start(f32[96,128]{1,0:T(8,128)S(1)} %get-tuple-element.55), channel_id=1, source_target_pairs={{0,4},{1,5},{2,6},{3,7},{4,0},{5,1},{6,2},{7,3},{8,12},{9,13},{10,... | collective-permute-start | bytes 147464 | tf_op jit(solution)/shard_map/ppermute | solution.py:755
  28.2 7.3 %collective-permute-start.13 = (f32[96,128]{1,0:T(8,128)S(1)}, f32[96,128]{1,0:T(8,128)S(1)}, u32[]{:S(2)}, u32[]{:S(2)}) collective-permute-start(f32[96,128]{1,0:T(8,128)S(1)} %get-tuple-element.56), channel_id=1, source_target_pairs={{0,1},{1,0},{2,29},{3,30},{4,9},{5,10},{6,11},{7,15},{8,16},{9,4},... | collective-permute-start | bytes 147464 | tf_op jit(solution)/shard_map/ppermute | solution.py:755
  29.5 6.0 %collective-permute-start.14 = (f32[96,128]{1,0:T(8,128)S(1)}, f32[96,128]{1,0:T(8,128)S(1)}, u32[]{:S(2)}, u32[]{:S(2)}) collective-permute-start(f32[96,128]{1,0:T(8,128)S(1)} %get-tuple-element.57), channel_id=1, source_target_pairs={{0,8},{1,4},{2,5},{3,6},{4,1},{5,2},{6,3},{7,15},{8,0},{9,12},{10,... | collective-permute-start | bytes 147464 | tf_op jit(solution)/shard_map/ppermute | solution.py:755
  30.4 5.3 %collective-permute-start.15 = (f32[96,128]{1,0:T(8,128)S(1)}, f32[96,128]{1,0:T(8,128)S(1)}, u32[]{:S(2)}, u32[]{:S(2)}) collective-permute-start(f32[96,128]{1,0:T(8,128)S(1)} %get-tuple-element.58), channel_id=1, source_target_pairs={{0,29},{1,30},{2,31},{3,11},{4,12},{5,8},{6,9},{7,10},{8,5},{9,6},... | collective-permute-start | bytes 147464 | tf_op jit(solution)/shard_map/ppermute | solution.py:755
  32.7 4.4 %collective-permute-start.16 = (f32[96,128]{1,0:T(8,128)S(1)}, f32[96,128]{1,0:T(8,128)S(1)}, u32[]{:S(2)}, u32[]{:S(2)}) collective-permute-start(f32[96,128]{1,0:T(8,128)S(1)} %get-tuple-element.59), channel_id=1, source_target_pairs={{0,28},{1,29},{2,30},{3,31},{4,8},{5,9},{6,10},{7,11},{8,4},{9,5},... | collective-permute-start | bytes 147464 | tf_op jit(solution)/shard_map/ppermute | solution.py:755
  32.7 4.4 %collective-permute-start.17 = (f32[96,128]{1,0:T(8,128)S(1)}, f32[96,128]{1,0:T(8,128)S(1)}, u32[]{:S(2)}, u32[]{:S(2)}) collective-permute-start(f32[96,128]{1,0:T(8,128)S(1)} %get-tuple-element.60), channel_id=1, source_target_pairs={{0,5},{1,6},{2,7},{3,11},{4,12},{5,0},{6,1},{7,2},{8,13},{9,14},{1... | collective-permute-start | bytes 147464 | tf_op jit(solution)/shard_map/ppermute | solution.py:755
where the time goes:
time: 39.8 us; the launch traced here: 39.7 us
  starting transfers between devices  21.8 us (55%)
  Pallas kernels  12.8 us (32%)
  waiting for transfers between devices  3.32 us (8%)
  between operations  1.76 us (4%)
    ppermute x18, starting transfers between devices, exchange(): lax.ppermute(payloads[k], ('gx', 'gy'), routes[i])  21.8 us
    pallas_call x7, Pallas kernels, run(): pl.pallas_call(body, out_shape=[jax.ShapeDtypeStruct(s, jnp.float32) if i...  12.8 us
    ppermute x18, waiting for transfers between devices, exchange(): lax.ppermute(payloads[k], ('gx', 'gy'), routes[i])  3.32 us
  transfers between devices with their start and end apart: 18, of which 4 were waited for; matrix products, arithmetic and copies ran while one was open for 0% of the time, Pallas kernels for 12%

commit v1 on v0

--- a/solution.py
+++ b/solution.py
@@ -17,7 +17,7 @@
 STENCIL = (-490.0, 270.0, -27.0, 2.0)
 BLEND = ((1.5, -0.15, 1.0 / 90.0), (-0.15, 1.0 / 90.0, 0.0), (1.0 / 90.0, 0.0, 0.0))
 SHIFTS = (-1, 0, 1)
-ORDER = (1, 5, 0, 3, 4, 2)
+ORDER = (0, 5, 2, 3, 4, 1)
 CHUNK = 512
 BF16 = ml_dtypes.bfloat16
 
@@ -126,9 +126,6 @@
     while len(rest) > 1:
         x, y = rest.pop(0)
         mate = min(rest, key=lambda d: (abs(d[1] - y) + abs(d[0] // 2 - x // 2), d))
-        if parity == 1 and x == 0:
-            wrapped = [d for d in rest if d == (nx - 1, y - across)]
-            mate = wrapped[0] if wrapped else mate
         rest.remove(mate)
         taken[(x, y)] = mate
         taken[mate] = (x, y)

time: 39.8 us -> 37.9 us (0.952); the launches traced: 39.7 us -> 37.2 us
  waiting for transfers between devices: 3.32 us -> 0.48 us
    ppermute x18, waiting for transfers between devices: 3.32 us -> 0.48 us  [exchange(): lax.ppermute(payloads[k], ('gx', 'gy'), routes[i])]
  transfers between devices with their start and end apart: 18 -> 18, of which waited for: 4 -> 3; matrix products, arithmetic and copies ran while one was open for 0% -> 0% of each run, Pallas kernels for 12% -> 21%
where the time goes in v1:
time: 37.9 us; the launch traced here: 37.2 us
  starting transfers between devices  22.1 us (58%)
  Pallas kernels  12.8 us (34%)
  between operations  1.75 us (5%)
  waiting for transfers between devices  0.48 us (1%)
    ppermute x18, starting transfers between devices, exchange(): lax.ppermute(payloads[k], ('gx', 'gy'), routes[i])  22.1 us
    pallas_call x7, Pallas kernels, run(): pl.pallas_call(body, out_shape=[jax.ShapeDtypeStruct(s, jnp.float32) if i...  12.8 us
  transfers between devices with their start and end apart: 18, of which 3 were waited for; matrix products, arithmetic and copies ran while one was open for 0% of the time, Pallas kernels for 21%

profile of v1, /device:TPU:0, one launch (start us, length us, event | category | flops | bytes accessed | tf_op | source)
XLA Modules:
  0.0 37.2 jit_solution(2463514530706478314)
XLA Ops:
  1.3 0.0 copy-start.1
  1.3 0.0 copy-start.3
  1.3 0.0 copy-start.4
  1.3 0.0 copy-start.6
  1.4 0.0 copy-start.7
  1.4 0.0 copy-start.10
  1.4 2.5 %shard_map.185 = (f32[96,128]{1,0:T(8,128)S(1)}, f32[96,128]{1,0:T(8,128)S(1)}, f32[96,128]{1,0:T(8,128)S(1)}, f32[96,128]{1,0:T(8,128)S(1)}, f32[96,128]{1,0:T(...) custom-call(s32[1]{0:T(128)S(6)} %copy.26.flags.flag.refs_0_, ...), custom_call_target="tpu_custom_call" | custom-call | bytes 6422584 | tf_op jit(solution)/shard_map/pallas_call | solution.py:717
  3.9 3.6 %collective-permute-start = (f32[96,128]{1,0:T(8,128)S(1)}, f32[96,128]{1,0:T(8,128)S(1)}, u32[]{:S(2)}, u32[]{:S(2)}) collective-permute-start(f32[96,128]{1,0:T(8,128)S(1)} %get-tuple-element.36), channel_id=1, source_target_pairs={{0,8},{1,4},{2,5},{3,6},{4,1},{5,2},{6,3},{7,15},{8,0},{9,12},{10,... | collective-permute-start | bytes 147464 | tf_op jit(solution)/shard_map/ppermute | solution.py:752
  7.6 0.2 collective-permute-start.1
  7.7 2.0 %collective-permute-start.2 = (f32[96,128]{1,0:T(8,128)S(1)}, f32[96,128]{1,0:T(8,128)S(1)}, u32[]{:S(2)}, u32[]{:S(2)}) collective-permute-start(f32[96,128]{1,0:T(8,128)S(1)} %get-tuple-element.38), channel_id=1, source_target_pairs={{0,5},{1,6},{2,7},{3,11},{4,12},{5,0},{6,1},{7,2},{8,13},{9,14},{1... | collective-permute-start | bytes 147464 | tf_op jit(solution)/shard_map/ppermute | solution.py:752
  9.8 0.2 collective-permute-start.3
  10.0 1.7 %collective-permute-start.4 = (f32[96,128]{1,0:T(8,128)S(1)}, f32[96,128]{1,0:T(8,128)S(1)}, u32[]{:S(2)}, u32[]{:S(2)}) collective-permute-start(f32[96,128]{1,0:T(8,128)S(1)} %get-tuple-element.40), channel_id=1, source_target_pairs={{0,1},{1,0},{2,3},{3,2},{4,8},{5,9},{6,10},{7,11},{8,4},{9,5},{10,... | collective-permute-start | bytes 147464 | tf_op jit(solution)/shard_map/ppermute | solution.py:752
  11.7 0.0 collective-permute-done.refs_3_
  11.7 0.0 collective-permute-start.5
  11.8 0.0 copy-start.2
  11.8 0.0 copy-start.5
  11.8 0.0 copy-start.9
  11.8 0.0 copy-start.12
  11.8 0.0 copy-start
  11.8 0.0 copy-start.8
  11.8 0.0 copy-start.11
  11.8 2.3 %shard_map.186 = (f32[128,4096]{1,0:T(8,128)S(1)}, f32[192,128]{1,0:T(8,128)S(1)}) custom-call(s32[1]{0:T(128)S(6)} %copy.26.flags.flag.refs_0_, f32[128,4096]{1,0:T(8,128)S(1)} %get-tuple-element.42.whole.before, f32[128,4096]{1,0:T(8,128)S(1)} %get-tuple-element.43.before, f32[128,4096]{1,0:T(8,128)S(1)} %get-tuple-element.44.cosine, ...), custom_call_target="tpu_custom_call" | custom-call | flops 1000000000 | bytes 6750212 | tf_op jit(solution)/shard_map/pallas_call | solution.py:717
  14.2 0.0 collective-permute-done.1.refs_4_
  14.2 0.0 collective-permute-done.2.refs_5_
  14.2 0.1 collective-permute-done.4.refs_7_
  14.3 0.0 collective-permute-done.5.refs_8_
  14.3 0.5 %shard_map.187 = (f32[192,128]{1,0:T(8,128)S(1)}, f32[96,128]{1,0:T(8,128)S(1)}, f32[96,128]{1,0:T(8,128)S(1)}, f32[96,128]{1,0:T(8,128)S(1)}, f32[96,128]{1,0:T...) custom-call(s32[1]{0:T(128)S(6)} %copy.26.flags.flag.refs_0_, s32[1]{0:T(128)} %bitcast.place.refs_1_, ...), custom_call_target="tpu_custom_call" | custom-call | bytes 843784 | tf_op jit(solution)/shard_map/pallas_call | solution.py:717
  14.8 2.7 %collective-permute-start.6 = (f32[96,128]{1,0:T(8,128)S(1)}, f32[96,128]{1,0:T(8,128)S(1)}, u32[]{:S(2)}, u32[]{:S(2)}) collective-permute-start(f32[96,128]{1,0:T(8,128)S(1)} %get-tuple-element.46), channel_id=1, source_target_pairs={{0,8},{1,4},{2,5},{3,6},{4,1},{5,2},{6,3},{7,15},{8,0},{9,12},{10,... | collective-permute-start | bytes 147464 | tf_op jit(solution)/shard_map/ppermute | solution.py:752
  17.5 0.0 collective-permute-start.7
  17.5 3.5 %collective-permute-start.8 = (f32[96,128]{1,0:T(8,128)S(1)}, f32[96,128]{1,0:T(8,128)S(1)}, u32[]{:S(2)}, u32[]{:S(2)}) collective-permute-start(f32[96,128]{1,0:T(8,128)S(1)} %get-tuple-element.48), channel_id=1, source_target_pairs={{0,5},{1,6},{2,7},{3,11},{4,12},{5,0},{6,1},{7,2},{8,13},{9,14},{1... | collective-permute-start | bytes 147464 | tf_op jit(solution)/shard_map/ppermute | solution.py:752
  21.1 0.3 collective-permute-start.9
  21.4 0.7 %collective-permute-start.10 = (f32[96,128]{1,0:T(8,128)S(1)}, f32[96,128]{1,0:T(8,128)S(1)}, u32[]{:S(2)}, u32[]{:S(2)}) collective-permute-start(f32[96,128]{1,0:T(8,128)S(1)} %get-tuple-element.50), channel_id=1, source_target_pairs={{0,1},{1,0},{2,3},{3,2},{4,8},{5,9},{6,10},{7,11},{8,4},{9,5},{10,... | collective-permute-start | bytes 147464 | tf_op jit(solution)/shard_map/ppermute | solution.py:752
  22.1 0.0 collective-permute-done.6.refs_3_
  22.1 0.5 %collective-permute-start.11 = (f32[96,128]{1,0:T(8,128)S(1)}, f32[96,128]{1,0:T(8,128)S(1)}, u32[]{:S(2)}, u32[]{:S(2)}) collective-permute-start(f32[96,128]{1,0:T(8,128)S(1)} %get-tuple-element.51), channel_id=1, source_target_pairs={{0,4},{1,5},{2,6},{3,7},{4,0},{5,1},{6,2},{7,3},{8,12},{9,13},{10,... | collective-permute-start | bytes 147464 | tf_op jit(solution)/shard_map/ppermute | solution.py:752
  22.7 2.6 %shard_map.188 = (f32[128,4096]{1,0:T(8,128)S(1)}, f32[128,4096]{1,0:T(8,128)S(1)}, f32[192,128]{1,0:T(8,128)S(1)}) custom-call(s32[1]{0:T(128)S(6)} %copy.26.flags.flag.refs_0_, f32[192,128]{1,0:T(8,128)S(1)} %get-tuple-element.52.forces, f32[128,4096]{1,0:T(8,128)S(1)} %get-tuple-element.53._, ...), custom_call_target="tpu_custom_call", output_to_operand_aliasing={{0}: (2, {})} | custom-call | flops 1000000000 | bytes 8962052 | tf_op jit(solution)/shard_map/pallas_call | solution.py:717
  25.3 0.0 collective-permute-done.7.refs_4_
  25.3 0.2 collective-permute-done.10.refs_7_
  25.5 0.5 %shard_map.189 = (f32[192,128]{1,0:T(8,128)S(1)}, f32[96,128]{1,0:T(8,128)S(1)}, f32[96,128]{1,0:T(8,128)S(1)}, f32[96,128]{1,0:T(8,128)S(1)}, f32[96,128]{1,0:T...) custom-call(s32[1]{0:T(128)S(6)} %copy.26.flags.flag.refs_0_, s32[1]{0:T(128)} %bitcast.place.refs_1_, ...), custom_call_target="tpu_custom_call" | custom-call | bytes 843784 | tf_op jit(solution)/shard_map/pallas_call | solution.py:717
  26.0 1.9 %collective-permute-start.12 = (f32[96,128]{1,0:T(8,128)S(1)}, f32[96,128]{1,0:T(8,128)S(1)}, u32[]{:S(2)}, u32[]{:S(2)}) collective-permute-start(f32[96,128]{1,0:T(8,128)S(1)} %get-tuple-element.55), channel_id=1, source_target_pairs={{0,8},{1,4},{2,5},{3,6},{4,1},{5,2},{6,3},{7,15},{8,0},{9,12},{10,... | collective-permute-start | bytes 147464 | tf_op jit(solution)/shard_map/ppermute | solution.py:752
  27.9 0.6 %collective-permute-start.13 = (f32[96,128]{1,0:T(8,128)S(1)}, f32[96,128]{1,0:T(8,128)S(1)}, u32[]{:S(2)}, u32[]{:S(2)}) collective-permute-start(f32[96,128]{1,0:T(8,128)S(1)} %get-tuple-element.56), channel_id=1, source_target_pairs={{0,1},{1,0},{2,3},{3,2},{4,9},{5,10},{6,11},{7,15},{8,16},{9,4},{1... | collective-permute-start | bytes 147464 | tf_op jit(solution)/shard_map/ppermute | solution.py:752
  28.5 2.4 %collective-permute-start.14 = (f32[96,128]{1,0:T(8,128)S(1)}, f32[96,128]{1,0:T(8,128)S(1)}, u32[]{:S(2)}, u32[]{:S(2)}) collective-permute-start(f32[96,128]{1,0:T(8,128)S(1)} %get-tuple-element.57), channel_id=1, source_target_pairs={{0,5},{1,6},{2,7},{3,11},{4,12},{5,0},{6,1},{7,2},{8,13},{9,14},{1... | collective-permute-start | bytes 147464 | tf_op jit(solution)/shard_map/ppermute | solution.py:752
  30.9 0.5 %collective-permute-start.15 = (f32[96,128]{1,0:T(8,128)S(1)}, f32[96,128]{1,0:T(8,128)S(1)}, u32[]{:S(2)}, u32[]{:S(2)}) collective-permute-start(f32[96,128]{1,0:T(8,128)S(1)} %get-tuple-element.58), channel_id=1, source_target_pairs={{0,4},{1,2},{2,1},{3,11},{4,0},{5,8},{6,9},{7,10},{8,5},{9,6},{10,... | collective-permute-start | bytes 147464 | tf_op jit(solution)/shard_map/ppermute | solution.py:752
  31.4 0.7 %collective-permute-start.16 = (f32[96,128]{1,0:T(8,128)S(1)}, f32[96,128]{1,0:T(8,128)S(1)}, u32[]{:S(2)}, u32[]{:S(2)}) collective-permute-start(f32[96,128]{1,0:T(8,128)S(1)} %get-tuple-element.59), channel_id=1, source_target_pairs={{0,1},{1,0},{2,3},{3,2},{4,8},{5,9},{6,10},{7,11},{8,4},{9,5},{10,... | collective-permute-start | bytes 147464 | tf_op jit(solution)/shard_map/ppermute | solution.py:752
  32.2 0.3 collective-permute-start.17
  32.5 2.8 %shard_map.190 = (f32[128,4096]{1,0:T(8,128)S(1)}, f32[128,4096]{1,0:T(8,128)S(1)}, f32[192,128]{1,0:T(8,128)S(1)}) custom-call(s32[1]{0:T(128)S(6)} %copy.26.flags.flag.refs_0_, f32[192,128]{1,0:T(8,128)S(1)} %get-tuple-element.61.forces, f32[128,4096]{1,0:T(8,128)S(1)} %get-tuple-element.62._, ...), custom_call_target="tpu_custom_call", output_to_operand_aliasing={{0}: (2, {})} | custom-call | flops 1000000000 | bytes 8962052 | tf_op jit(solution)/shard_map/pallas_call | solution.py:717
  35.3 0.0 collective-permute-done.13.refs_4_
  35.3 0.2 collective-permute-done.16.refs_7_
  35.5 1.6 %shard_map.191 = (f32[1,128,4096]{2,1,0:T(8,128)}, f32[192,128]{1,0:T(8,128)}) custom-call(s32[1]{0:T(128)S(6)} %copy.26.flags.flag.refs_0_, s32[1]{0:T(128)} %bitcast.place.refs_1_, s32[8,128]{1,0:T(8,128)S(1)} %get-tuple-element.35.refs_2_, f32[96,128]{1,0:T(8,128)S(1)} %collective-permute-done.12.refs_3_, f32[96,128]{1,0:T(8,128)S(1)} %collective-permute-done.13.refs_4_, ...), custom_call_target="tpu_custom_call" | custom-call | bytes 5054472 | tf_op jit(solution)/shard_map/pallas_call | solution.py:717
  (21 shorter events, 0.0 us)
Async XLA Ops:
  1.3 10.4 %copy-start.1 = (bf16[384,128]{1,0:T(8,128)(2,1)S(1)}, bf16[384,128]{1,0:T(8,128)(2,1)}, u32[]{:S(2)}) copy-start(bf16[384,128]{1,0:T(8,128)(2,1)} %constant.68.clone.refs_2_.refs_14_) | copy-start | bytes 294916
  1.3 10.4 %copy-start.3 = (f32[384,128]{1,0:T(8,128)S(1)}, f32[384,128]{1,0:T(8,128)}, u32[]{:S(2)}) copy-start(f32[384,128]{1,0:T(8,128)} %constant.69.clone.refs_3_) | copy-start | bytes 589828
  1.3 10.4 %copy-start.4 = (bf16[64,192]{1,0:T(8,128)(2,1)S(1)}, bf16[64,192]{1,0:T(8,128)(2,1)}, u32[]{:S(2)}) copy-start(bf16[64,192]{1,0:T(8,128)(2,1)} %constant.67.clone.refs_1_.refs_13_) | copy-start | bytes 73732
  1.3 10.4 %copy-start.6 = (bf16[128,256]{1,0:T(8,128)(2,1)S(1)}, bf16[128,256]{1,0:T(8,128)(2,1)}, u32[]{:S(2)}) copy-start(bf16[128,256]{1,0:T(8,128)(2,1)} %constant.71.clone.refs_4_) | copy-start | bytes 196612
  1.4 10.4 %copy-start.7 = (bf16[256,128]{1,0:T(8,128)(2,1)S(1)}, bf16[256,128]{1,0:T(8,128)(2,1)}, u32[]{:S(2)}) copy-start(bf16[256,128]{1,0:T(8,128)(2,1)} %constant.72.clone.refs_5_) | copy-start | bytes 196612
  1.4 10.4 %copy-start.10 = (bf16[16,256]{1,0:T(8,128)(2,1)S(1)}, bf16[16,256]{1,0:T(8,128)(2,1)}, u32[]{:S(2)}) copy-start(bf16[16,256]{1,0:T(8,128)(2,1)} %constant.62.clone.refs_0_) | copy-start | bytes 24580
  3.9 7.8 %collective-permute-start = (f32[96,128]{1,0:T(8,128)S(1)}, f32[96,128]{1,0:T(8,128)S(1)}, u32[]{:S(2)}, u32[]{:S(2)}) collective-permute-start(f32[96,128]{1,0:T(8,128)S(1)} %get-tuple-element.36), channel_id=1, source_target_pairs={{0,8},{1,4},{2,5},{3,6},{4,1},{5,2},{6,3},{7,15},{8,0},{9,12},{10,... | collective-permute-start | bytes 147464 | tf_op jit(solution)/shard_map/ppermute | solution.py:752
  7.6 6.6 %collective-permute-start.1 = (f32[96,128]{1,0:T(8,128)S(1)}, f32[96,128]{1,0:T(8,128)S(1)}, u32[]{:S(2)}, u32[]{:S(2)}) collective-permute-start(f32[96,128]{1,0:T(8,128)S(1)} %get-tuple-element.37), channel_id=1, source_target_pairs={{0,1},{1,0},{2,3},{3,2},{4,9},{5,10},{6,11},{7,15},{8,16},{9,4},{1... | collective-permute-start | bytes 147464 | tf_op jit(solution)/shard_map/ppermute | solution.py:752
  7.7 6.5 %collective-permute-start.2 = (f32[96,128]{1,0:T(8,128)S(1)}, f32[96,128]{1,0:T(8,128)S(1)}, u32[]{:S(2)}, u32[]{:S(2)}) collective-permute-start(f32[96,128]{1,0:T(8,128)S(1)} %get-tuple-element.38), channel_id=1, source_target_pairs={{0,5},{1,6},{2,7},{3,11},{4,12},{5,0},{6,1},{7,2},{8,13},{9,14},{1... | collective-permute-start | bytes 147464 | tf_op jit(solution)/shard_map/ppermute | solution.py:752
  9.8 4.4 %collective-permute-start.3 = (f32[96,128]{1,0:T(8,128)S(1)}, f32[96,128]{1,0:T(8,128)S(1)}, u32[]{:S(2)}, u32[]{:S(2)}) collective-permute-start(f32[96,128]{1,0:T(8,128)S(1)} %get-tuple-element.39), channel_id=1, source_target_pairs={{0,4},{1,2},{2,1},{3,11},{4,0},{5,8},{6,9},{7,10},{8,5},{9,6},{10,... | collective-permute-start | bytes 147464 | tf_op jit(solution)/shard_map/ppermute | solution.py:752
  10.0 4.3 %collective-permute-start.4 = (f32[96,128]{1,0:T(8,128)S(1)}, f32[96,128]{1,0:T(8,128)S(1)}, u32[]{:S(2)}, u32[]{:S(2)}) collective-permute-start(f32[96,128]{1,0:T(8,128)S(1)} %get-tuple-element.40), channel_id=1, source_target_pairs={{0,1},{1,0},{2,3},{3,2},{4,8},{5,9},{6,10},{7,11},{8,4},{9,5},{10,... | collective-permute-start | bytes 147464 | tf_op jit(solution)/shard_map/ppermute | solution.py:752
  11.7 2.6 %collective-permute-start.5 = (f32[96,128]{1,0:T(8,128)S(1)}, f32[96,128]{1,0:T(8,128)S(1)}, u32[]{:S(2)}, u32[]{:S(2)}) collective-permute-start(f32[96,128]{1,0:T(8,128)S(1)} %get-tuple-element.41), channel_id=1, source_target_pairs={{0,4},{1,5},{2,6},{3,7},{4,0},{5,1},{6,2},{7,3},{8,12},{9,13},{10,... | collective-permute-start | bytes 147464 | tf_op jit(solution)/shard_map/ppermute | solution.py:752
  11.8 2.5 %copy-start.2 = (f32[384,128]{1,0:T(8,128)S(1)}, f32[384,128]{1,0:T(8,128)}, u32[]{:S(2)}) copy-start(f32[384,128]{1,0:T(8,128)} %constant.64.clone.refs_10_) | copy-start | bytes 589828
  11.8 2.5 %copy-start.5 = (bf16[384,128]{1,0:T(8,128)(2,1)S(1)}, bf16[384,128]{1,0:T(8,128)(2,1)}, u32[]{:S(2)}) copy-start(bf16[384,128]{1,0:T(8,128)(2,1)} %constant.66.clone.refs_12_) | copy-start | bytes 294916
  11.8 2.5 %copy-start.9 = (bf16[64,192]{1,0:T(8,128)(2,1)S(1)}, bf16[64,192]{1,0:T(8,128)(2,1)}, u32[]{:S(2)}) copy-start(bf16[64,192]{1,0:T(8,128)(2,1)} %constant.65.clone.refs_11_) | copy-start | bytes 73732
  11.8 2.5 %copy-start.12 = (f32[8,128]{1,0:T(8,128)S(1)}, f32[8,128]{1,0:T(8,128)}, u32[]{:S(2)}) copy-start(f32[8,128]{1,0:T(8,128)} %constant.73.clone.refs_15_) | copy-start | bytes 12292
  11.8 10.9 %copy-start = (f32[128,4096]{1,0:T(8,128)S(1)}, f32[128,4096]{1,0:T(8,128)}, u32[]{:S(2)}) copy-start(f32[128,4096]{1,0:T(8,128)} %constant.61.clone.gain.refs_17_) | copy-start | bytes 6291460
  11.8 10.9 %copy-start.8 = (bf16[128,32]{1,0:T(8,128)(2,1)S(1)}, bf16[128,32]{1,0:T(8,128)(2,1)}, u32[]{:S(2)}) copy-start(bf16[128,32]{1,0:T(8,128)(2,1)} %constant.63.clone.inject.refs_18_) | copy-start | bytes 24580
  11.8 10.8 %copy-start.11 = (f32[16,128]{1,0:T(8,128)S(1)}, f32[16,128]{1,0:T(8,128)}, u32[]{:S(2)}) copy-start(f32[16,128]{1,0:T(8,128)} %constant.70.clone.ends.refs_19_) | copy-start | bytes 24580
  14.8 7.3 %collective-permute-start.6 = (f32[96,128]{1,0:T(8,128)S(1)}, f32[96,128]{1,0:T(8,128)S(1)}, u32[]{:S(2)}, u32[]{:S(2)}) collective-permute-start(f32[96,128]{1,0:T(8,128)S(1)} %get-tuple-element.46), channel_id=1, source_target_pairs={{0,8},{1,4},{2,5},{3,6},{4,1},{5,2},{6,3},{7,15},{8,0},{9,12},{10,... | collective-permute-start | bytes 147464 | tf_op jit(solution)/shard_map/ppermute | solution.py:752
  17.5 7.8 %collective-permute-start.7 = (f32[96,128]{1,0:T(8,128)S(1)}, f32[96,128]{1,0:T(8,128)S(1)}, u32[]{:S(2)}, u32[]{:S(2)}) collective-permute-start(f32[96,128]{1,0:T(8,128)S(1)} %get-tuple-element.47), channel_id=1, source_target_pairs={{0,1},{1,0},{2,3},{3,2},{4,9},{5,10},{6,11},{7,15},{8,16},{9,4},{1... | collective-permute-start | bytes 147464 | tf_op jit(solution)/shard_map/ppermute | solution.py:752
  17.5 7.8 %collective-permute-start.8 = (f32[96,128]{1,0:T(8,128)S(1)}, f32[96,128]{1,0:T(8,128)S(1)}, u32[]{:S(2)}, u32[]{:S(2)}) collective-permute-start(f32[96,128]{1,0:T(8,128)S(1)} %get-tuple-element.48), channel_id=1, source_target_pairs={{0,5},{1,6},{2,7},{3,11},{4,12},{5,0},{6,1},{7,2},{8,13},{9,14},{1... | collective-permute-start | bytes 147464 | tf_op jit(solution)/shard_map/ppermute | solution.py:752
  21.1 4.3 %collective-permute-start.9 = (f32[96,128]{1,0:T(8,128)S(1)}, f32[96,128]{1,0:T(8,128)S(1)}, u32[]{:S(2)}, u32[]{:S(2)}) collective-permute-start(f32[96,128]{1,0:T(8,128)S(1)} %get-tuple-element.49), channel_id=1, source_target_pairs={{0,4},{1,2},{2,1},{3,11},{4,0},{5,8},{6,9},{7,10},{8,5},{9,6},{10,... | collective-permute-start | bytes 147464 | tf_op jit(solution)/shard_map/ppermute | solution.py:752
  21.4 4.1 %collective-permute-start.10 = (f32[96,128]{1,0:T(8,128)S(1)}, f32[96,128]{1,0:T(8,128)S(1)}, u32[]{:S(2)}, u32[]{:S(2)}) collective-permute-start(f32[96,128]{1,0:T(8,128)S(1)} %get-tuple-element.50), channel_id=1, source_target_pairs={{0,1},{1,0},{2,3},{3,2},{4,8},{5,9},{6,10},{7,11},{8,4},{9,5},{10,... | collective-permute-start | bytes 147464 | tf_op jit(solution)/shard_map/ppermute | solution.py:752
  22.1 3.4 %collective-permute-start.11 = (f32[96,128]{1,0:T(8,128)S(1)}, f32[96,128]{1,0:T(8,128)S(1)}, u32[]{:S(2)}, u32[]{:S(2)}) collective-permute-start(f32[96,128]{1,0:T(8,128)S(1)} %get-tuple-element.51), channel_id=1, source_target_pairs={{0,4},{1,5},{2,6},{3,7},{4,0},{5,1},{6,2},{7,3},{8,12},{9,13},{10,... | collective-permute-start | bytes 147464 | tf_op jit(solution)/shard_map/ppermute | solution.py:752
  26.0 6.2 %collective-permute-start.12 = (f32[96,128]{1,0:T(8,128)S(1)}, f32[96,128]{1,0:T(8,128)S(1)}, u32[]{:S(2)}, u32[]{:S(2)}) collective-permute-start(f32[96,128]{1,0:T(8,128)S(1)} %get-tuple-element.55), channel_id=1, source_target_pairs={{0,8},{1,4},{2,5},{3,6},{4,1},{5,2},{6,3},{7,15},{8,0},{9,12},{10,... | collective-permute-start | bytes 147464 | tf_op jit(solution)/shard_map/ppermute | solution.py:752
  27.9 7.3 %collective-permute-start.13 = (f32[96,128]{1,0:T(8,128)S(1)}, f32[96,128]{1,0:T(8,128)S(1)}, u32[]{:S(2)}, u32[]{:S(2)}) collective-permute-start(f32[96,128]{1,0:T(8,128)S(1)} %get-tuple-element.56), channel_id=1, source_target_pairs={{0,1},{1,0},{2,3},{3,2},{4,9},{5,10},{6,11},{7,15},{8,16},{9,4},{1... | collective-permute-start | bytes 147464 | tf_op jit(solution)/shard_map/ppermute | solution.py:752
  28.5 6.8 %collective-permute-start.14 = (f32[96,128]{1,0:T(8,128)S(1)}, f32[96,128]{1,0:T(8,128)S(1)}, u32[]{:S(2)}, u32[]{:S(2)}) collective-permute-start(f32[96,128]{1,0:T(8,128)S(1)} %get-tuple-element.57), channel_id=1, source_target_pairs={{0,5},{1,6},{2,7},{3,11},{4,12},{5,0},{6,1},{7,2},{8,13},{9,14},{1... | collective-permute-start | bytes 147464 | tf_op jit(solution)/shard_map/ppermute | solution.py:752
  30.9 4.4 %collective-permute-start.15 = (f32[96,128]{1,0:T(8,128)S(1)}, f32[96,128]{1,0:T(8,128)S(1)}, u32[]{:S(2)}, u32[]{:S(2)}) collective-permute-start(f32[96,128]{1,0:T(8,128)S(1)} %get-tuple-element.58), channel_id=1, source_target_pairs={{0,4},{1,2},{2,1},{3,11},{4,0},{5,8},{6,9},{7,10},{8,5},{9,6},{10,... | collective-permute-start | bytes 147464 | tf_op jit(solution)/shard_map/ppermute | solution.py:752
  31.4 4.1 %collective-permute-start.16 = (f32[96,128]{1,0:T(8,128)S(1)}, f32[96,128]{1,0:T(8,128)S(1)}, u32[]{:S(2)}, u32[]{:S(2)}) collective-permute-start(f32[96,128]{1,0:T(8,128)S(1)} %get-tuple-element.59), channel_id=1, source_target_pairs={{0,1},{1,0},{2,3},{3,2},{4,8},{5,9},{6,10},{7,11},{8,4},{9,5},{10,... | collective-permute-start | bytes 147464 | tf_op jit(solution)/shard_map/ppermute | solution.py:752
  32.2 3.4 %collective-permute-start.17 = (f32[96,128]{1,0:T(8,128)S(1)}, f32[96,128]{1,0:T(8,128)S(1)}, u32[]{:S(2)}, u32[]{:S(2)}) collective-permute-start(f32[96,128]{1,0:T(8,128)S(1)} %get-tuple-element.60), channel_id=1, source_target_pairs={{0,4},{1,5},{2,6},{3,7},{4,0},{5,1},{6,2},{7,3},{8,12},{9,13},{10,... | collective-permute-start | bytes 147464 | tf_op jit(solution)/shard_map/ppermute | solution.py:752

commit v2 on v1

--- a/solution.py
+++ b/solution.py
@@ -490,7 +490,7 @@
     collect, inverse_one, inverse_two = refs[9:]
     total = held.shape[1]
     tiles = total // 128
-    spans = strips(held, 2 * CHUNK)
+    spans = strips(held)
     first = copies([(listed, rows)], sems)
     tables = copies(zip(sources, (collect, inverse_one, inverse_two)), sems, 1)
     moves = copies([(now.at[0, :, p], held.at[:, p]) for p in spans], sems, 4)

time: 37.9 us -> 37.5 us (0.989)
  the two profiles are of different devices: /device:TPU:0 before, /device:TPU:4 now
where the time goes in v2:
time: 37.5 us; the launch traced here: 37.3 us
  starting transfers between devices  15 us (40%)
  Pallas kernels  12.8 us (34%)
  waiting for transfers between devices  7.61 us (20%)
  between operations  1.76 us (5%)
    ppermute x18, starting transfers between devices, exchange(): lax.ppermute(payloads[k], ('gx', 'gy'), routes[i])  15 us
    pallas_call x7, Pallas kernels, run(): pl.pallas_call(body, out_shape=[jax.ShapeDtypeStruct(s, jnp.float32) if i...  12.8 us
    ppermute x18, waiting for transfers between devices, exchange(): lax.ppermute(payloads[k], ('gx', 'gy'), routes[i])  7.61 us
  transfers between devices with their start and end apart: 18, of which 7 were waited for; matrix products, arithmetic and copies ran while one was open for 0% of the time, Pallas kernels for 12%

profile of v2, /device:TPU:4, one launch (start us, length us, event | category | flops | bytes accessed | tf_op | source)
XLA Modules:
  0.0 37.3 jit_solution(11081370618636200434)
XLA Ops:
  1.3 0.0 copy-start.1
  1.3 0.0 copy-start.3
  1.3 0.0 copy-start.4
  1.3 0.0 copy-start.6
  1.4 0.0 copy-start.7
  1.4 0.0 copy-start.10
  1.4 3.2 %shard_map.185 = (f32[96,128]{1,0:T(8,128)S(1)}, f32[96,128]{1,0:T(8,128)S(1)}, f32[96,128]{1,0:T(8,128)S(1)}, f32[96,128]{1,0:T(8,128)S(1)}, f32[96,128]{1,0:T(...) custom-call(s32[1]{0:T(128)S(6)} %copy.26.flags.flag.refs_0_, ...), custom_call_target="tpu_custom_call" | custom-call | bytes 6422584 | tf_op jit(solution)/shard_map/pallas_call | solution.py:717
  4.6 0.9 %collective-permute-start = (f32[96,128]{1,0:T(8,128)S(1)}, f32[96,128]{1,0:T(8,128)S(1)}, u32[]{:S(2)}, u32[]{:S(2)}) collective-permute-start(f32[96,128]{1,0:T(8,128)S(1)} %get-tuple-element.36), channel_id=1, source_target_pairs={{0,8},{1,4},{2,5},{3,6},{4,1},{5,2},{6,3},{7,15},{8,0},{9,12},{10,... | collective-permute-start | bytes 147464 | tf_op jit(solution)/shard_map/ppermute | solution.py:752
  5.5 0.0 collective-permute-start.1
  5.5 3.0 %collective-permute-start.2 = (f32[96,128]{1,0:T(8,128)S(1)}, f32[96,128]{1,0:T(8,128)S(1)}, u32[]{:S(2)}, u32[]{:S(2)}) collective-permute-start(f32[96,128]{1,0:T(8,128)S(1)} %get-tuple-element.38), channel_id=1, source_target_pairs={{0,5},{1,6},{2,7},{3,11},{4,12},{5,0},{6,1},{7,2},{8,13},{9,14},{1... | collective-permute-start | bytes 147464 | tf_op jit(solution)/shard_map/ppermute | solution.py:752
  8.5 1.0 %collective-permute-start.3 = (f32[96,128]{1,0:T(8,128)S(1)}, f32[96,128]{1,0:T(8,128)S(1)}, u32[]{:S(2)}, u32[]{:S(2)}) collective-permute-start(f32[96,128]{1,0:T(8,128)S(1)} %get-tuple-element.39), channel_id=1, source_target_pairs={{0,4},{1,2},{2,1},{3,11},{4,0},{5,8},{6,9},{7,10},{8,5},{9,6},{10,... | collective-permute-start | bytes 147464 | tf_op jit(solution)/shard_map/ppermute | solution.py:752
  9.6 0.2 collective-permute-start.4
  9.8 0.0 collective-permute-done.refs_3_
  9.8 0.6 %collective-permute-start.5 = (f32[96,128]{1,0:T(8,128)S(1)}, f32[96,128]{1,0:T(8,128)S(1)}, u32[]{:S(2)}, u32[]{:S(2)}) collective-permute-start(f32[96,128]{1,0:T(8,128)S(1)} %get-tuple-element.41), channel_id=1, source_target_pairs={{0,4},{1,5},{2,6},{3,7},{4,0},{5,1},{6,2},{7,3},{8,12},{9,13},{10,... | collective-permute-start | bytes 147464 | tf_op jit(solution)/shard_map/ppermute | solution.py:752
  10.5 0.0 copy-start.2
  10.5 0.0 copy-start.5
  10.5 0.0 copy-start.9
  10.5 0.0 copy-start.12
  10.5 0.0 copy-start
  10.5 0.0 copy-start.8
  10.6 0.0 copy-start.11
  10.6 1.2 %shard_map.186 = (f32[128,4096]{1,0:T(8,128)S(1)}, f32[192,128]{1,0:T(8,128)S(1)}) custom-call(s32[1]{0:T(128)S(6)} %copy.26.flags.flag.refs_0_, f32[128,4096]{1,0:T(8,128)S(1)} %get-tuple-element.42.whole.before, f32[128,4096]{1,0:T(8,128)S(1)} %get-tuple-element.43.before, f32[128,4096]{1,0:T(8,128)S(1)} %get-tuple-element.44.cosine, ...), custom_call_target="tpu_custom_call" | custom-call | flops 1000000000 | bytes 6750212 | tf_op jit(solution)/shard_map/pallas_call | solution.py:717
  11.8 0.0 collective-permute-done.2.refs_5_
  11.8 2.1 %collective-permute-done.3.refs_6_ = f32[96,128]{1,0:T(8,128)S(1)} collective-permute-done((f32[96,128]{1,0:T(8,128)S(1)}, f32[96,128]{1,0:T(8,128)S(1)}, u32[]{:S(2)}, u32[]{:S(2)}) %collective-permute-start.3) | collective-permute-done | bytes 49184 | tf_op jit(solution)/shard_map/ppermute | solution.py:752
  13.9 0.5 %collective-permute-done.4.refs_7_ = f32[96,128]{1,0:T(8,128)S(1)} collective-permute-done((f32[96,128]{1,0:T(8,128)S(1)}, f32[96,128]{1,0:T(8,128)S(1)}, u32[]{:S(2)}, u32[]{:S(2)}) %collective-permute-start.4) | collective-permute-done | bytes 49184 | tf_op jit(solution)/shard_map/ppermute | solution.py:752
  14.4 1.3 %shard_map.187 = (f32[192,128]{1,0:T(8,128)S(1)}, f32[96,128]{1,0:T(8,128)S(1)}, f32[96,128]{1,0:T(8,128)S(1)}, f32[96,128]{1,0:T(8,128)S(1)}, f32[96,128]{1,0:T...) custom-call(s32[1]{0:T(128)S(6)} %copy.26.flags.flag.refs_0_, s32[1]{0:T(128)} %bitcast.place.refs_1_, ...), custom_call_target="tpu_custom_call" | custom-call | bytes 843784 | tf_op jit(solution)/shard_map/pallas_call | solution.py:717
  15.7 0.1 collective-permute-start.6
  15.8 0.1 collective-permute-start.7
  15.9 2.0 %collective-permute-start.8 = (f32[96,128]{1,0:T(8,128)S(1)}, f32[96,128]{1,0:T(8,128)S(1)}, u32[]{:S(2)}, u32[]{:S(2)}) collective-permute-start(f32[96,128]{1,0:T(8,128)S(1)} %get-tuple-element.48), channel_id=1, source_target_pairs={{0,5},{1,6},{2,7},{3,11},{4,12},{5,0},{6,1},{7,2},{8,13},{9,14},{1... | collective-permute-start | bytes 147464 | tf_op jit(solution)/shard_map/ppermute | solution.py:752
  17.9 2.4 %collective-permute-start.9 = (f32[96,128]{1,0:T(8,128)S(1)}, f32[96,128]{1,0:T(8,128)S(1)}, u32[]{:S(2)}, u32[]{:S(2)}) collective-permute-start(f32[96,128]{1,0:T(8,128)S(1)} %get-tuple-element.49), channel_id=1, source_target_pairs={{0,4},{1,2},{2,1},{3,11},{4,0},{5,8},{6,9},{7,10},{8,5},{9,6},{10,... | collective-permute-start | bytes 147464 | tf_op jit(solution)/shard_map/ppermute | solution.py:752
  20.2 0.0 collective-permute-start.10
  20.3 1.7 %shard_map.188 = (f32[128,4096]{1,0:T(8,128)S(1)}, f32[128,4096]{1,0:T(8,128)S(1)}, f32[192,128]{1,0:T(8,128)S(1)}) custom-call(s32[1]{0:T(128)S(6)} %copy.26.flags.flag.refs_0_, f32[192,128]{1,0:T(8,128)S(1)} %get-tuple-element.52.forces, f32[128,4096]{1,0:T(8,128)S(1)} %get-tuple-element.53._, ...), custom_call_target="tpu_custom_call", output_to_operand_aliasing={{0}: (2, {})} | custom-call | flops 1000000000 | bytes 8962052 | tf_op jit(solution)/shard_map/pallas_call | solution.py:717
  22.0 0.0 collective-permute-done.7.refs_4_
  22.0 0.0 collective-permute-done.8.refs_5_
  22.0 1.3 %collective-permute-done.9.refs_6_ = f32[96,128]{1,0:T(8,128)S(1)} collective-permute-done((f32[96,128]{1,0:T(8,128)S(1)}, f32[96,128]{1,0:T(8,128)S(1)}, u32[]{:S(2)}, u32[]{:S(2)}) %collective-permute-start.9) | collective-permute-done | bytes 49184 | tf_op jit(solution)/shard_map/ppermute | solution.py:752
  23.3 1.4 %collective-permute-done.10.refs_7_ = f32[96,128]{1,0:T(8,128)S(1)} collective-permute-done((f32[96,128]{1,0:T(8,128)S(1)}, f32[96,128]{1,0:T(8,128)S(1)}, u32[]{:S(2)}, u32[]{:S(2)}) %collective-permute-start.10) | collective-permute-done | bytes 49184 | tf_op jit(solution)/shard_map/ppermute | solution.py:752
  24.7 1.3 %shard_map.189 = (f32[192,128]{1,0:T(8,128)S(1)}, f32[96,128]{1,0:T(8,128)S(1)}, f32[96,128]{1,0:T(8,128)S(1)}, f32[96,128]{1,0:T(8,128)S(1)}, f32[96,128]{1,0:T...) custom-call(s32[1]{0:T(128)S(6)} %copy.26.flags.flag.refs_0_, s32[1]{0:T(128)} %bitcast.place.refs_1_, ...), custom_call_target="tpu_custom_call" | custom-call | bytes 843784 | tf_op jit(solution)/shard_map/pallas_call | solution.py:717
  25.9 0.1 collective-permute-start.12
  26.0 0.6 %collective-permute-start.13 = (f32[96,128]{1,0:T(8,128)S(1)}, f32[96,128]{1,0:T(8,128)S(1)}, u32[]{:S(2)}, u32[]{:S(2)}) collective-permute-start(f32[96,128]{1,0:T(8,128)S(1)} %get-tuple-element.56), channel_id=1, source_target_pairs={{0,1},{1,0},{2,3},{3,2},{4,9},{5,10},{6,11},{7,15},{8,16},{9,4},{1... | collective-permute-start | bytes 147464 | tf_op jit(solution)/shard_map/ppermute | solution.py:752
  26.6 0.8 %collective-permute-start.14 = (f32[96,128]{1,0:T(8,128)S(1)}, f32[96,128]{1,0:T(8,128)S(1)}, u32[]{:S(2)}, u32[]{:S(2)}) collective-permute-start(f32[96,128]{1,0:T(8,128)S(1)} %get-tuple-element.57), channel_id=1, source_target_pairs={{0,5},{1,6},{2,7},{3,11},{4,12},{5,0},{6,1},{7,2},{8,13},{9,14},{1... | collective-permute-start | bytes 147464 | tf_op jit(solution)/shard_map/ppermute | solution.py:752
  27.4 2.8 %collective-permute-start.15 = (f32[96,128]{1,0:T(8,128)S(1)}, f32[96,128]{1,0:T(8,128)S(1)}, u32[]{:S(2)}, u32[]{:S(2)}) collective-permute-start(f32[96,128]{1,0:T(8,128)S(1)} %get-tuple-element.58), channel_id=1, source_target_pairs={{0,4},{1,2},{2,1},{3,11},{4,0},{5,8},{6,9},{7,10},{8,5},{9,6},{10,... | collective-permute-start | bytes 147464 | tf_op jit(solution)/shard_map/ppermute | solution.py:752
  30.2 0.3 collective-permute-start.16
  30.5 0.3 collective-permute-done.12.refs_3_
  30.8 0.0 collective-permute-start.17
  30.8 1.7 %shard_map.190 = (f32[128,4096]{1,0:T(8,128)S(1)}, f32[128,4096]{1,0:T(8,128)S(1)}, f32[192,128]{1,0:T(8,128)S(1)}) custom-call(s32[1]{0:T(128)S(6)} %copy.26.flags.flag.refs_0_, f32[192,128]{1,0:T(8,128)S(1)} %get-tuple-element.61.forces, f32[128,4096]{1,0:T(8,128)S(1)} %get-tuple-element.62._, ...), custom_call_target="tpu_custom_call", output_to_operand_aliasing={{0}: (2, {})} | custom-call | flops 1000000000 | bytes 8962052 | tf_op jit(solution)/shard_map/pallas_call | solution.py:717
  32.6 0.2 collective-permute-done.15.refs_6_
  32.8 1.8 %collective-permute-done.16.refs_7_ = f32[96,128]{1,0:T(8,128)S(1)} collective-permute-done((f32[96,128]{1,0:T(8,128)S(1)}, f32[96,128]{1,0:T(8,128)S(1)}, u32[]{:S(2)}, u32[]{:S(2)}) %collective-permute-start.16) | collective-permute-done | bytes 49184 | tf_op jit(solution)/shard_map/ppermute | solution.py:752
  34.6 2.5 %shard_map.191 = (f32[1,128,4096]{2,1,0:T(8,128)}, f32[192,128]{1,0:T(8,128)}) custom-call(s32[1]{0:T(128)S(6)} %copy.26.flags.flag.refs_0_, s32[1]{0:T(128)} %bitcast.place.refs_1_, s32[8,128]{1,0:T(8,128)S(1)} %get-tuple-element.35.refs_2_, f32[96,128]{1,0:T(8,128)S(1)} %collective-permute-done.12.refs_3_, f32[96,128]{1,0:T(8,128)S(1)} %collective-permute-done.13.refs_4_, ...), custom_call_target="tpu_custom_call" | custom-call | bytes 5054472 | tf_op jit(solution)/shard_map/pallas_call | solution.py:717
  (21 shorter events, 0.0 us)
Async XLA Ops:
  1.3 9.1 %copy-start.1 = (bf16[384,128]{1,0:T(8,128)(2,1)S(1)}, bf16[384,128]{1,0:T(8,128)(2,1)}, u32[]{:S(2)}) copy-start(bf16[384,128]{1,0:T(8,128)(2,1)} %constant.68.clone.refs_2_.refs_14_) | copy-start | bytes 294916
  1.3 9.1 %copy-start.3 = (f32[384,128]{1,0:T(8,128)S(1)}, f32[384,128]{1,0:T(8,128)}, u32[]{:S(2)}) copy-start(f32[384,128]{1,0:T(8,128)} %constant.69.clone.refs_3_) | copy-start | bytes 589828
  1.3 9.1 %copy-start.4 = (bf16[64,192]{1,0:T(8,128)(2,1)S(1)}, bf16[64,192]{1,0:T(8,128)(2,1)}, u32[]{:S(2)}) copy-start(bf16[64,192]{1,0:T(8,128)(2,1)} %constant.67.clone.refs_1_.refs_13_) | copy-start | bytes 73732
  1.3 9.1 %copy-start.6 = (bf16[128,256]{1,0:T(8,128)(2,1)S(1)}, bf16[128,256]{1,0:T(8,128)(2,1)}, u32[]{:S(2)}) copy-start(bf16[128,256]{1,0:T(8,128)(2,1)} %constant.71.clone.refs_4_) | copy-start | bytes 196612
  1.4 9.1 %copy-start.7 = (bf16[256,128]{1,0:T(8,128)(2,1)S(1)}, bf16[256,128]{1,0:T(8,128)(2,1)}, u32[]{:S(2)}) copy-start(bf16[256,128]{1,0:T(8,128)(2,1)} %constant.72.clone.refs_5_) | copy-start | bytes 196612
  1.4 9.1 %copy-start.10 = (bf16[16,256]{1,0:T(8,128)(2,1)S(1)}, bf16[16,256]{1,0:T(8,128)(2,1)}, u32[]{:S(2)}) copy-start(bf16[16,256]{1,0:T(8,128)(2,1)} %constant.62.clone.refs_0_) | copy-start | bytes 24580
  4.6 5.2 %collective-permute-start = (f32[96,128]{1,0:T(8,128)S(1)}, f32[96,128]{1,0:T(8,128)S(1)}, u32[]{:S(2)}, u32[]{:S(2)}) collective-permute-start(f32[96,128]{1,0:T(8,128)S(1)} %get-tuple-element.36), channel_id=1, source_target_pairs={{0,8},{1,4},{2,5},{3,6},{4,1},{5,2},{6,3},{7,15},{8,0},{9,12},{10,... | collective-permute-start | bytes 147464 | tf_op jit(solution)/shard_map/ppermute | solution.py:752
  5.5 6.3 %collective-permute-start.1 = (f32[96,128]{1,0:T(8,128)S(1)}, f32[96,128]{1,0:T(8,128)S(1)}, u32[]{:S(2)}, u32[]{:S(2)}) collective-permute-start(f32[96,128]{1,0:T(8,128)S(1)} %get-tuple-element.37), channel_id=1, source_target_pairs={{0,1},{1,0},{2,3},{3,2},{4,9},{5,10},{6,11},{7,15},{8,16},{9,4},{1... | collective-permute-start | bytes 147464 | tf_op jit(solution)/shard_map/ppermute | solution.py:752
  5.5 6.3 %collective-permute-start.2 = (f32[96,128]{1,0:T(8,128)S(1)}, f32[96,128]{1,0:T(8,128)S(1)}, u32[]{:S(2)}, u32[]{:S(2)}) collective-permute-start(f32[96,128]{1,0:T(8,128)S(1)} %get-tuple-element.38), channel_id=1, source_target_pairs={{0,5},{1,6},{2,7},{3,11},{4,12},{5,0},{6,1},{7,2},{8,13},{9,14},{1... | collective-permute-start | bytes 147464 | tf_op jit(solution)/shard_map/ppermute | solution.py:752
  8.5 5.4 %collective-permute-start.3 = (f32[96,128]{1,0:T(8,128)S(1)}, f32[96,128]{1,0:T(8,128)S(1)}, u32[]{:S(2)}, u32[]{:S(2)}) collective-permute-start(f32[96,128]{1,0:T(8,128)S(1)} %get-tuple-element.39), channel_id=1, source_target_pairs={{0,4},{1,2},{2,1},{3,11},{4,0},{5,8},{6,9},{7,10},{8,5},{9,6},{10,... | collective-permute-start | bytes 147464 | tf_op jit(solution)/shard_map/ppermute | solution.py:752
  9.6 4.8 %collective-permute-start.4 = (f32[96,128]{1,0:T(8,128)S(1)}, f32[96,128]{1,0:T(8,128)S(1)}, u32[]{:S(2)}, u32[]{:S(2)}) collective-permute-start(f32[96,128]{1,0:T(8,128)S(1)} %get-tuple-element.40), channel_id=1, source_target_pairs={{0,1},{1,0},{2,3},{3,2},{4,8},{5,9},{6,10},{7,11},{8,4},{9,5},{10,... | collective-permute-start | bytes 147464 | tf_op jit(solution)/shard_map/ppermute | solution.py:752
  9.8 4.6 %collective-permute-start.5 = (f32[96,128]{1,0:T(8,128)S(1)}, f32[96,128]{1,0:T(8,128)S(1)}, u32[]{:S(2)}, u32[]{:S(2)}) collective-permute-start(f32[96,128]{1,0:T(8,128)S(1)} %get-tuple-element.41), channel_id=1, source_target_pairs={{0,4},{1,5},{2,6},{3,7},{4,0},{5,1},{6,2},{7,3},{8,12},{9,13},{10,... | collective-permute-start | bytes 147464 | tf_op jit(solution)/shard_map/ppermute | solution.py:752
  10.5 3.9 %copy-start.2 = (f32[384,128]{1,0:T(8,128)S(1)}, f32[384,128]{1,0:T(8,128)}, u32[]{:S(2)}) copy-start(f32[384,128]{1,0:T(8,128)} %constant.64.clone.refs_10_) | copy-start | bytes 589828
  10.5 3.9 %copy-start.5 = (bf16[384,128]{1,0:T(8,128)(2,1)S(1)}, bf16[384,128]{1,0:T(8,128)(2,1)}, u32[]{:S(2)}) copy-start(bf16[384,128]{1,0:T(8,128)(2,1)} %constant.66.clone.refs_12_) | copy-start | bytes 294916
  10.5 3.9 %copy-start.9 = (bf16[64,192]{1,0:T(8,128)(2,1)S(1)}, bf16[64,192]{1,0:T(8,128)(2,1)}, u32[]{:S(2)}) copy-start(bf16[64,192]{1,0:T(8,128)(2,1)} %constant.65.clone.refs_11_) | copy-start | bytes 73732
  10.5 3.9 %copy-start.12 = (f32[8,128]{1,0:T(8,128)S(1)}, f32[8,128]{1,0:T(8,128)}, u32[]{:S(2)}) copy-start(f32[8,128]{1,0:T(8,128)} %constant.73.clone.refs_15_) | copy-start | bytes 12292
  10.5 9.7 %copy-start = (f32[128,4096]{1,0:T(8,128)S(1)}, f32[128,4096]{1,0:T(8,128)}, u32[]{:S(2)}) copy-start(f32[128,4096]{1,0:T(8,128)} %constant.61.clone.gain.refs_17_) | copy-start | bytes 6291460
  10.5 9.7 %copy-start.8 = (bf16[128,32]{1,0:T(8,128)(2,1)S(1)}, bf16[128,32]{1,0:T(8,128)(2,1)}, u32[]{:S(2)}) copy-start(bf16[128,32]{1,0:T(8,128)(2,1)} %constant.63.clone.inject.refs_18_) | copy-start | bytes 24580
  10.6 9.7 %copy-start.11 = (f32[16,128]{1,0:T(8,128)S(1)}, f32[16,128]{1,0:T(8,128)}, u32[]{:S(2)}) copy-start(f32[16,128]{1,0:T(8,128)} %constant.70.clone.ends.refs_19_) | copy-start | bytes 24580
  15.7 4.6 %collective-permute-start.6 = (f32[96,128]{1,0:T(8,128)S(1)}, f32[96,128]{1,0:T(8,128)S(1)}, u32[]{:S(2)}, u32[]{:S(2)}) collective-permute-start(f32[96,128]{1,0:T(8,128)S(1)} %get-tuple-element.46), channel_id=1, source_target_pairs={{0,8},{1,4},{2,5},{3,6},{4,1},{5,2},{6,3},{7,15},{8,0},{9,12},{10,... | collective-permute-start | bytes 147464 | tf_op jit(solution)/shard_map/ppermute | solution.py:752
  15.8 6.2 %collective-permute-start.7 = (f32[96,128]{1,0:T(8,128)S(1)}, f32[96,128]{1,0:T(8,128)S(1)}, u32[]{:S(2)}, u32[]{:S(2)}) collective-permute-start(f32[96,128]{1,0:T(8,128)S(1)} %get-tuple-element.47), channel_id=1, source_target_pairs={{0,1},{1,0},{2,3},{3,2},{4,9},{5,10},{6,11},{7,15},{8,16},{9,4},{1... | collective-permute-start | bytes 147464 | tf_op jit(solution)/shard_map/ppermute | solution.py:752
  15.9 6.2 %collective-permute-start.8 = (f32[96,128]{1,0:T(8,128)S(1)}, f32[96,128]{1,0:T(8,128)S(1)}, u32[]{:S(2)}, u32[]{:S(2)}) collective-permute-start(f32[96,128]{1,0:T(8,128)S(1)} %get-tuple-element.48), channel_id=1, source_target_pairs={{0,5},{1,6},{2,7},{3,11},{4,12},{5,0},{6,1},{7,2},{8,13},{9,14},{1... | collective-permute-start | bytes 147464 | tf_op jit(solution)/shard_map/ppermute | solution.py:752
  17.9 5.4 %collective-permute-start.9 = (f32[96,128]{1,0:T(8,128)S(1)}, f32[96,128]{1,0:T(8,128)S(1)}, u32[]{:S(2)}, u32[]{:S(2)}) collective-permute-start(f32[96,128]{1,0:T(8,128)S(1)} %get-tuple-element.49), channel_id=1, source_target_pairs={{0,4},{1,2},{2,1},{3,11},{4,0},{5,8},{6,9},{7,10},{8,5},{9,6},{10,... | collective-permute-start | bytes 147464 | tf_op jit(solution)/shard_map/ppermute | solution.py:752
  20.2 4.4 %collective-permute-start.10 = (f32[96,128]{1,0:T(8,128)S(1)}, f32[96,128]{1,0:T(8,128)S(1)}, u32[]{:S(2)}, u32[]{:S(2)}) collective-permute-start(f32[96,128]{1,0:T(8,128)S(1)} %get-tuple-element.50), channel_id=1, source_target_pairs={{0,1},{1,0},{2,3},{3,2},{4,8},{5,9},{6,10},{7,11},{8,4},{9,5},{10,... | collective-permute-start | bytes 147464 | tf_op jit(solution)/shard_map/ppermute | solution.py:752
  20.3 4.4 %collective-permute-start.11 = (f32[96,128]{1,0:T(8,128)S(1)}, f32[96,128]{1,0:T(8,128)S(1)}, u32[]{:S(2)}, u32[]{:S(2)}) collective-permute-start(f32[96,128]{1,0:T(8,128)S(1)} %get-tuple-element.51), channel_id=1, source_target_pairs={{0,4},{1,5},{2,6},{3,7},{4,0},{5,1},{6,2},{7,3},{8,12},{9,13},{10,... | collective-permute-start | bytes 147464 | tf_op jit(solution)/shard_map/ppermute | solution.py:752
  25.9 4.9 %collective-permute-start.12 = (f32[96,128]{1,0:T(8,128)S(1)}, f32[96,128]{1,0:T(8,128)S(1)}, u32[]{:S(2)}, u32[]{:S(2)}) collective-permute-start(f32[96,128]{1,0:T(8,128)S(1)} %get-tuple-element.55), channel_id=1, source_target_pairs={{0,8},{1,4},{2,5},{3,6},{4,1},{5,2},{6,3},{7,15},{8,0},{9,12},{10,... | collective-permute-start | bytes 147464 | tf_op jit(solution)/shard_map/ppermute | solution.py:752
  26.0 6.5 %collective-permute-start.13 = (f32[96,128]{1,0:T(8,128)S(1)}, f32[96,128]{1,0:T(8,128)S(1)}, u32[]{:S(2)}, u32[]{:S(2)}) collective-permute-start(f32[96,128]{1,0:T(8,128)S(1)} %get-tuple-element.56), channel_id=1, source_target_pairs={{0,1},{1,0},{2,3},{3,2},{4,9},{5,10},{6,11},{7,15},{8,16},{9,4},{1... | collective-permute-start | bytes 147464 | tf_op jit(solution)/shard_map/ppermute | solution.py:752
  26.6 5.9 %collective-permute-start.14 = (f32[96,128]{1,0:T(8,128)S(1)}, f32[96,128]{1,0:T(8,128)S(1)}, u32[]{:S(2)}, u32[]{:S(2)}) collective-permute-start(f32[96,128]{1,0:T(8,128)S(1)} %get-tuple-element.57), channel_id=1, source_target_pairs={{0,5},{1,6},{2,7},{3,11},{4,12},{5,0},{6,1},{7,2},{8,13},{9,14},{1... | collective-permute-start | bytes 147464 | tf_op jit(solution)/shard_map/ppermute | solution.py:752
  27.4 5.4 %collective-permute-start.15 = (f32[96,128]{1,0:T(8,128)S(1)}, f32[96,128]{1,0:T(8,128)S(1)}, u32[]{:S(2)}, u32[]{:S(2)}) collective-permute-start(f32[96,128]{1,0:T(8,128)S(1)} %get-tuple-element.58), channel_id=1, source_target_pairs={{0,4},{1,2},{2,1},{3,11},{4,0},{5,8},{6,9},{7,10},{8,5},{9,6},{10,... | collective-permute-start | bytes 147464 | tf_op jit(solution)/shard_map/ppermute | solution.py:752
  30.2 4.4 %collective-permute-start.16 = (f32[96,128]{1,0:T(8,128)S(1)}, f32[96,128]{1,0:T(8,128)S(1)}, u32[]{:S(2)}, u32[]{:S(2)}) collective-permute-start(f32[96,128]{1,0:T(8,128)S(1)} %get-tuple-element.59), channel_id=1, source_target_pairs={{0,1},{1,0},{2,3},{3,2},{4,8},{5,9},{6,10},{7,11},{8,4},{9,5},{10,... | collective-permute-start | bytes 147464 | tf_op jit(solution)/shard_map/ppermute | solution.py:752
  30.8 3.8 %collective-permute-start.17 = (f32[96,128]{1,0:T(8,128)S(1)}, f32[96,128]{1,0:T(8,128)S(1)}, u32[]{:S(2)}, u32[]{:S(2)}) collective-permute-start(f32[96,128]{1,0:T(8,128)S(1)} %get-tuple-element.60), channel_id=1, source_target_pairs={{0,4},{1,5},{2,6},{3,7},{4,0},{5,1},{6,2},{7,3},{8,12},{9,13},{10,... | collective-permute-start | bytes 147464 | tf_op jit(solution)/shard_map/ppermute | solution.py:752

commit v3 on v2

--- a/solution.py
+++ b/solution.py
@@ -680,8 +680,9 @@
     def _():
         modes = mirrored_forward(push, forward_one, forward_two)
         spread_modal_forces(modes, gathered)
-        show(modal_layers(modes, layers, coupled, inverse_one, inverse_two))
-        for m, p in zip(moves, broad):
+        for i, (m, p) in enumerate(zip(moves, broad)):
+            if i == len(broad) // 2:
+                show(modal_layers(modes, layers, coupled, inverse_one, inverse_two))
             moved = injected(gathered, inject, p.start, 2 * CHUNK)
             held[:, p] = free[:, p] + gain[:, p] * moved
             m.start()

time: 37.5 us -> 37.7 us (level)
  the two profiles are of different devices: /device:TPU:4 before, /device:TPU:0 now
where the time goes in v3:
time: 37.7 us; the launch traced here: 37.6 us
  starting transfers between devices  19.5 us (52%)
  Pallas kernels  12.7 us (34%)
  waiting for transfers between devices  3.5 us (9%)
  between operations  1.77 us (5%)
    ppermute x18, starting transfers between devices, exchange(): lax.ppermute(payloads[k], ('gx', 'gy'), routes[i])  19.5 us
    pallas_call x7, Pallas kernels, run(): pl.pallas_call(body, out_shape=[jax.ShapeDtypeStruct(s, jnp.float32) if i...  12.7 us
    ppermute x18, waiting for transfers between devices, exchange(): lax.ppermute(payloads[k], ('gx', 'gy'), routes[i])  3.5 us
  transfers between devices with their start and end apart: 18, of which 3 were waited for; matrix products, arithmetic and copies ran while one was open for 0% of the time, Pallas kernels for 12%

profile of v3, /device:TPU:0, one launch (start us, length us, event | category | flops | bytes accessed | tf_op | source)
XLA Modules:
  0.0 37.6 jit_solution(16224113799089880095)
XLA Ops:
  1.3 0.0 copy-start.1
  1.3 0.0 copy-start.3
  1.3 0.0 copy-start.4
  1.3 0.0 copy-start.6
  1.4 0.0 copy-start.7
  1.4 0.0 copy-start.10
  1.4 3.2 %shard_map.185 = (f32[96,128]{1,0:T(8,128)S(1)}, f32[96,128]{1,0:T(8,128)S(1)}, f32[96,128]{1,0:T(8,128)S(1)}, f32[96,128]{1,0:T(8,128)S(1)}, f32[96,128]{1,0:T(...) custom-call(s32[1]{0:T(128)S(6)} %copy.26.flags.flag.refs_0_, ...), custom_call_target="tpu_custom_call" | custom-call | bytes 6422584 | tf_op jit(solution)/shard_map/pallas_call | solution.py:718
  4.6 3.0 %collective-permute-start = (f32[96,128]{1,0:T(8,128)S(1)}, f32[96,128]{1,0:T(8,128)S(1)}, u32[]{:S(2)}, u32[]{:S(2)}) collective-permute-start(f32[96,128]{1,0:T(8,128)S(1)} %get-tuple-element.36), channel_id=1, source_target_pairs={{0,8},{1,4},{2,5},{3,6},{4,1},{5,2},{6,3},{7,15},{8,0},{9,12},{10,... | collective-permute-start | bytes 147464 | tf_op jit(solution)/shard_map/ppermute | solution.py:753
  7.6 0.2 collective-permute-start.1
  7.8 2.2 %collective-permute-start.2 = (f32[96,128]{1,0:T(8,128)S(1)}, f32[96,128]{1,0:T(8,128)S(1)}, u32[]{:S(2)}, u32[]{:S(2)}) collective-permute-start(f32[96,128]{1,0:T(8,128)S(1)} %get-tuple-element.38), channel_id=1, source_target_pairs={{0,5},{1,6},{2,7},{3,11},{4,12},{5,0},{6,1},{7,2},{8,13},{9,14},{1... | collective-permute-start | bytes 147464 | tf_op jit(solution)/shard_map/ppermute | solution.py:753
  10.0 0.0 collective-permute-start.3
  10.0 1.8 %collective-permute-start.4 = (f32[96,128]{1,0:T(8,128)S(1)}, f32[96,128]{1,0:T(8,128)S(1)}, u32[]{:S(2)}, u32[]{:S(2)}) collective-permute-start(f32[96,128]{1,0:T(8,128)S(1)} %get-tuple-element.40), channel_id=1, source_target_pairs={{0,1},{1,0},{2,3},{3,2},{4,8},{5,9},{6,10},{7,11},{8,4},{9,5},{10,... | collective-permute-start | bytes 147464 | tf_op jit(solution)/shard_map/ppermute | solution.py:753
  11.7 0.0 collective-permute-done.refs_3_
  11.7 0.0 collective-permute-start.5
  11.8 0.0 copy-start.2
  11.8 0.0 copy-start.5
  11.8 0.0 copy-start.9
  11.8 0.0 copy-start.12
  11.9 0.0 copy-start
  11.9 0.0 copy-start.8
  11.9 0.0 copy-start.11
  11.9 1.2 %shard_map.186 = (f32[128,4096]{1,0:T(8,128)S(1)}, f32[192,128]{1,0:T(8,128)S(1)}) custom-call(s32[1]{0:T(128)S(6)} %copy.26.flags.flag.refs_0_, f32[128,4096]{1,0:T(8,128)S(1)} %get-tuple-element.42.whole.before, f32[128,4096]{1,0:T(8,128)S(1)} %get-tuple-element.43.before, f32[128,4096]{1,0:T(8,128)S(1)} %get-tuple-element.44.cosine, ...), custom_call_target="tpu_custom_call" | custom-call | flops 1000000000 | bytes 6750212 | tf_op jit(solution)/shard_map/pallas_call | solution.py:718
  13.1 0.0 collective-permute-done.1.refs_4_
  13.1 0.0 collective-permute-done.3.refs_6_
  13.1 1.2 %collective-permute-done.4.refs_7_ = f32[96,128]{1,0:T(8,128)S(1)} collective-permute-done((f32[96,128]{1,0:T(8,128)S(1)}, f32[96,128]{1,0:T(8,128)S(1)}, u32[]{:S(2)}, u32[]{:S(2)}) %collective-permute-start.4) | collective-permute-done | bytes 49184 | tf_op jit(solution)/shard_map/ppermute | solution.py:753
  14.4 1.3 %shard_map.187 = (f32[192,128]{1,0:T(8,128)S(1)}, f32[96,128]{1,0:T(8,128)S(1)}, f32[96,128]{1,0:T(8,128)S(1)}, f32[96,128]{1,0:T(8,128)S(1)}, f32[96,128]{1,0:T...) custom-call(s32[1]{0:T(128)S(6)} %copy.26.flags.flag.refs_0_, s32[1]{0:T(128)} %bitcast.place.refs_1_, ...), custom_call_target="tpu_custom_call" | custom-call | bytes 843784 | tf_op jit(solution)/shard_map/pallas_call | solution.py:718
  15.7 1.9 %collective-permute-start.6 = (f32[96,128]{1,0:T(8,128)S(1)}, f32[96,128]{1,0:T(8,128)S(1)}, u32[]{:S(2)}, u32[]{:S(2)}) collective-permute-start(f32[96,128]{1,0:T(8,128)S(1)} %get-tuple-element.46), channel_id=1, source_target_pairs={{0,8},{1,4},{2,5},{3,6},{4,1},{5,2},{6,3},{7,15},{8,0},{9,12},{10,... | collective-permute-start | bytes 147464 | tf_op jit(solution)/shard_map/ppermute | solution.py:753
  17.6 0.0 collective-permute-start.7
  17.6 3.6 %collective-permute-start.8 = (f32[96,128]{1,0:T(8,128)S(1)}, f32[96,128]{1,0:T(8,128)S(1)}, u32[]{:S(2)}, u32[]{:S(2)}) collective-permute-start(f32[96,128]{1,0:T(8,128)S(1)} %get-tuple-element.48), channel_id=1, source_target_pairs={{0,5},{1,6},{2,7},{3,11},{4,12},{5,0},{6,1},{7,2},{8,13},{9,14},{1... | collective-permute-start | bytes 147464 | tf_op jit(solution)/shard_map/ppermute | solution.py:753
  21.2 1.1 %collective-permute-start.10 = (f32[96,128]{1,0:T(8,128)S(1)}, f32[96,128]{1,0:T(8,128)S(1)}, u32[]{:S(2)}, u32[]{:S(2)}) collective-permute-start(f32[96,128]{1,0:T(8,128)S(1)} %get-tuple-element.50), channel_id=1, source_target_pairs={{0,1},{1,0},{2,3},{3,2},{4,8},{5,9},{6,10},{7,11},{8,4},{9,5},{10,... | collective-permute-start | bytes 147464 | tf_op jit(solution)/shard_map/ppermute | solution.py:753
  22.3 0.0 collective-permute-done.6.refs_3_
  22.3 0.5 %collective-permute-start.11 = (f32[96,128]{1,0:T(8,128)S(1)}, f32[96,128]{1,0:T(8,128)S(1)}, u32[]{:S(2)}, u32[]{:S(2)}) collective-permute-start(f32[96,128]{1,0:T(8,128)S(1)} %get-tuple-element.51), channel_id=1, source_target_pairs={{0,4},{1,5},{2,6},{3,7},{4,0},{5,1},{6,2},{7,3},{8,12},{9,13},{10,... | collective-permute-start | bytes 147464 | tf_op jit(solution)/shard_map/ppermute | solution.py:753
  22.8 1.7 %shard_map.188 = (f32[128,4096]{1,0:T(8,128)S(1)}, f32[128,4096]{1,0:T(8,128)S(1)}, f32[192,128]{1,0:T(8,128)S(1)}) custom-call(s32[1]{0:T(128)S(6)} %copy.26.flags.flag.refs_0_, f32[192,128]{1,0:T(8,128)S(1)} %get-tuple-element.52.forces, f32[128,4096]{1,0:T(8,128)S(1)} %get-tuple-element.53._, ...), custom_call_target="tpu_custom_call", output_to_operand_aliasing={{0}: (2, {})} | custom-call | flops 1000000000 | bytes 8962052 | tf_op jit(solution)/shard_map/pallas_call | solution.py:718
  24.4 0.0 collective-permute-done.7.refs_4_
  24.5 1.3 %collective-permute-done.10.refs_7_ = f32[96,128]{1,0:T(8,128)S(1)} collective-permute-done((f32[96,128]{1,0:T(8,128)S(1)}, f32[96,128]{1,0:T(8,128)S(1)}, u32[]{:S(2)}, u32[]{:S(2)}) %collective-permute-start.10) | collective-permute-done | bytes 49184 | tf_op jit(solution)/shard_map/ppermute | solution.py:753
  25.8 1.3 %shard_map.189 = (f32[192,128]{1,0:T(8,128)S(1)}, f32[96,128]{1,0:T(8,128)S(1)}, f32[96,128]{1,0:T(8,128)S(1)}, f32[96,128]{1,0:T(8,128)S(1)}, f32[96,128]{1,0:T...) custom-call(s32[1]{0:T(128)S(6)} %copy.26.flags.flag.refs_0_, s32[1]{0:T(128)} %bitcast.place.refs_1_, ...), custom_call_target="tpu_custom_call" | custom-call | bytes 843784 | tf_op jit(solution)/shard_map/pallas_call | solution.py:718
  27.0 1.5 %collective-permute-start.12 = (f32[96,128]{1,0:T(8,128)S(1)}, f32[96,128]{1,0:T(8,128)S(1)}, u32[]{:S(2)}, u32[]{:S(2)}) collective-permute-start(f32[96,128]{1,0:T(8,128)S(1)} %get-tuple-element.55), channel_id=1, source_target_pairs={{0,8},{1,4},{2,5},{3,6},{4,1},{5,2},{6,3},{7,15},{8,0},{9,12},{10,... | collective-permute-start | bytes 147464 | tf_op jit(solution)/shard_map/ppermute | solution.py:753
  28.6 0.0 collective-permute-start.13
  28.6 2.2 %collective-permute-start.14 = (f32[96,128]{1,0:T(8,128)S(1)}, f32[96,128]{1,0:T(8,128)S(1)}, u32[]{:S(2)}, u32[]{:S(2)}) collective-permute-start(f32[96,128]{1,0:T(8,128)S(1)} %get-tuple-element.57), channel_id=1, source_target_pairs={{0,5},{1,6},{2,7},{3,11},{4,12},{5,0},{6,1},{7,2},{8,13},{9,14},{1... | collective-permute-start | bytes 147464 | tf_op jit(solution)/shard_map/ppermute | solution.py:753
  30.8 1.4 %collective-permute-start.16 = (f32[96,128]{1,0:T(8,128)S(1)}, f32[96,128]{1,0:T(8,128)S(1)}, u32[]{:S(2)}, u32[]{:S(2)}) collective-permute-start(f32[96,128]{1,0:T(8,128)S(1)} %get-tuple-element.59), channel_id=1, source_target_pairs={{0,1},{1,0},{2,3},{3,2},{4,8},{5,9},{6,10},{7,11},{8,4},{9,5},{10,... | collective-permute-start | bytes 147464 | tf_op jit(solution)/shard_map/ppermute | solution.py:753
  32.2 0.0 collective-permute-done.12.refs_3_
  32.2 0.1 collective-permute-start.17
  32.4 1.7 %shard_map.190 = (f32[128,4096]{1,0:T(8,128)S(1)}, f32[128,4096]{1,0:T(8,128)S(1)}, f32[192,128]{1,0:T(8,128)S(1)}) custom-call(s32[1]{0:T(128)S(6)} %copy.26.flags.flag.refs_0_, f32[192,128]{1,0:T(8,128)S(1)} %get-tuple-element.61.forces, f32[128,4096]{1,0:T(8,128)S(1)} %get-tuple-element.62._, ...), custom_call_target="tpu_custom_call", output_to_operand_aliasing={{0}: (2, {})} | custom-call | flops 1000000000 | bytes 8962052 | tf_op jit(solution)/shard_map/pallas_call | solution.py:718
  34.1 0.0 collective-permute-done.14.refs_5_
  34.1 0.0 collective-permute-done.15.refs_6_
  34.1 1.0 %collective-permute-done.16.refs_7_ = f32[96,128]{1,0:T(8,128)S(1)} collective-permute-done((f32[96,128]{1,0:T(8,128)S(1)}, f32[96,128]{1,0:T(8,128)S(1)}, u32[]{:S(2)}, u32[]{:S(2)}) %collective-permute-start.16) | collective-permute-done | bytes 49184 | tf_op jit(solution)/shard_map/ppermute | solution.py:753
  35.1 0.0 collective-permute-done.17.refs_8_
  35.1 2.4 %shard_map.191 = (f32[1,128,4096]{2,1,0:T(8,128)}, f32[192,128]{1,0:T(8,128)}) custom-call(s32[1]{0:T(128)S(6)} %copy.26.flags.flag.refs_0_, s32[1]{0:T(128)} %bitcast.place.refs_1_, s32[8,128]{1,0:T(8,128)S(1)} %get-tuple-element.35.refs_2_, f32[96,128]{1,0:T(8,128)S(1)} %collective-permute-done.12.refs_3_, f32[96,128]{1,0:T(8,128)S(1)} %collective-permute-done.13.refs_4_, ...), custom_call_target="tpu_custom_call" | custom-call | bytes 5054472 | tf_op jit(solution)/shard_map/pallas_call | solution.py:718
  (21 shorter events, 0.0 us)
Async XLA Ops:
  1.3 10.4 %copy-start.1 = (bf16[384,128]{1,0:T(8,128)(2,1)S(1)}, bf16[384,128]{1,0:T(8,128)(2,1)}, u32[]{:S(2)}) copy-start(bf16[384,128]{1,0:T(8,128)(2,1)} %constant.68.clone.refs_2_.refs_14_) | copy-start | bytes 294916
  1.3 10.4 %copy-start.3 = (f32[384,128]{1,0:T(8,128)S(1)}, f32[384,128]{1,0:T(8,128)}, u32[]{:S(2)}) copy-start(f32[384,128]{1,0:T(8,128)} %constant.69.clone.refs_3_) | copy-start | bytes 589828
  1.3 10.4 %copy-start.4 = (bf16[64,192]{1,0:T(8,128)(2,1)S(1)}, bf16[64,192]{1,0:T(8,128)(2,1)}, u32[]{:S(2)}) copy-start(bf16[64,192]{1,0:T(8,128)(2,1)} %constant.67.clone.refs_1_.refs_13_) | copy-start | bytes 73732
  1.3 10.4 %copy-start.6 = (bf16[128,256]{1,0:T(8,128)(2,1)S(1)}, bf16[128,256]{1,0:T(8,128)(2,1)}, u32[]{:S(2)}) copy-start(bf16[128,256]{1,0:T(8,128)(2,1)} %constant.71.clone.refs_4_) | copy-start | bytes 196612
  1.4 10.4 %copy-start.7 = (bf16[256,128]{1,0:T(8,128)(2,1)S(1)}, bf16[256,128]{1,0:T(8,128)(2,1)}, u32[]{:S(2)}) copy-start(bf16[256,128]{1,0:T(8,128)(2,1)} %constant.72.clone.refs_5_) | copy-start | bytes 196612
  1.4 10.4 %copy-start.10 = (bf16[16,256]{1,0:T(8,128)(2,1)S(1)}, bf16[16,256]{1,0:T(8,128)(2,1)}, u32[]{:S(2)}) copy-start(bf16[16,256]{1,0:T(8,128)(2,1)} %constant.62.clone.refs_0_) | copy-start | bytes 24580
  4.6 7.2 %collective-permute-start = (f32[96,128]{1,0:T(8,128)S(1)}, f32[96,128]{1,0:T(8,128)S(1)}, u32[]{:S(2)}, u32[]{:S(2)}) collective-permute-start(f32[96,128]{1,0:T(8,128)S(1)} %get-tuple-element.36), channel_id=1, source_target_pairs={{0,8},{1,4},{2,5},{3,6},{4,1},{5,2},{6,3},{7,15},{8,0},{9,12},{10,... | collective-permute-start | bytes 147464 | tf_op jit(solution)/shard_map/ppermute | solution.py:753
  7.6 5.5 %collective-permute-start.1 = (f32[96,128]{1,0:T(8,128)S(1)}, f32[96,128]{1,0:T(8,128)S(1)}, u32[]{:S(2)}, u32[]{:S(2)}) collective-permute-start(f32[96,128]{1,0:T(8,128)S(1)} %get-tuple-element.37), channel_id=1, source_target_pairs={{0,1},{1,0},{2,3},{3,2},{4,9},{5,10},{6,11},{7,15},{8,16},{9,4},{1... | collective-permute-start | bytes 147464 | tf_op jit(solution)/shard_map/ppermute | solution.py:753
  7.8 5.4 %collective-permute-start.2 = (f32[96,128]{1,0:T(8,128)S(1)}, f32[96,128]{1,0:T(8,128)S(1)}, u32[]{:S(2)}, u32[]{:S(2)}) collective-permute-start(f32[96,128]{1,0:T(8,128)S(1)} %get-tuple-element.38), channel_id=1, source_target_pairs={{0,5},{1,6},{2,7},{3,11},{4,12},{5,0},{6,1},{7,2},{8,13},{9,14},{1... | collective-permute-start | bytes 147464 | tf_op jit(solution)/shard_map/ppermute | solution.py:753
  10.0 3.1 %collective-permute-start.3 = (f32[96,128]{1,0:T(8,128)S(1)}, f32[96,128]{1,0:T(8,128)S(1)}, u32[]{:S(2)}, u32[]{:S(2)}) collective-permute-start(f32[96,128]{1,0:T(8,128)S(1)} %get-tuple-element.39), channel_id=1, source_target_pairs={{0,4},{1,2},{2,1},{3,11},{4,0},{5,8},{6,9},{7,10},{8,5},{9,6},{10,... | collective-permute-start | bytes 147464 | tf_op jit(solution)/shard_map/ppermute | solution.py:753
  10.0 4.4 %collective-permute-start.4 = (f32[96,128]{1,0:T(8,128)S(1)}, f32[96,128]{1,0:T(8,128)S(1)}, u32[]{:S(2)}, u32[]{:S(2)}) collective-permute-start(f32[96,128]{1,0:T(8,128)S(1)} %get-tuple-element.40), channel_id=1, source_target_pairs={{0,1},{1,0},{2,3},{3,2},{4,8},{5,9},{6,10},{7,11},{8,4},{9,5},{10,... | collective-permute-start | bytes 147464 | tf_op jit(solution)/shard_map/ppermute | solution.py:753
  11.7 2.6 %collective-permute-start.5 = (f32[96,128]{1,0:T(8,128)S(1)}, f32[96,128]{1,0:T(8,128)S(1)}, u32[]{:S(2)}, u32[]{:S(2)}) collective-permute-start(f32[96,128]{1,0:T(8,128)S(1)} %get-tuple-element.41), channel_id=1, source_target_pairs={{0,4},{1,5},{2,6},{3,7},{4,0},{5,1},{6,2},{7,3},{8,12},{9,13},{10,... | collective-permute-start | bytes 147464 | tf_op jit(solution)/shard_map/ppermute | solution.py:753
  11.8 2.5 %copy-start.2 = (f32[384,128]{1,0:T(8,128)S(1)}, f32[384,128]{1,0:T(8,128)}, u32[]{:S(2)}) copy-start(f32[384,128]{1,0:T(8,128)} %constant.64.clone.refs_10_) | copy-start | bytes 589828
  11.8 2.5 %copy-start.5 = (bf16[384,128]{1,0:T(8,128)(2,1)S(1)}, bf16[384,128]{1,0:T(8,128)(2,1)}, u32[]{:S(2)}) copy-start(bf16[384,128]{1,0:T(8,128)(2,1)} %constant.66.clone.refs_12_) | copy-start | bytes 294916
  11.8 2.5 %copy-start.9 = (bf16[64,192]{1,0:T(8,128)(2,1)S(1)}, bf16[64,192]{1,0:T(8,128)(2,1)}, u32[]{:S(2)}) copy-start(bf16[64,192]{1,0:T(8,128)(2,1)} %constant.65.clone.refs_11_) | copy-start | bytes 73732
  11.8 2.5 %copy-start.12 = (f32[8,128]{1,0:T(8,128)S(1)}, f32[8,128]{1,0:T(8,128)}, u32[]{:S(2)}) copy-start(f32[8,128]{1,0:T(8,128)} %constant.73.clone.refs_15_) | copy-start | bytes 12292
  11.9 10.9 %copy-start = (f32[128,4096]{1,0:T(8,128)S(1)}, f32[128,4096]{1,0:T(8,128)}, u32[]{:S(2)}) copy-start(f32[128,4096]{1,0:T(8,128)} %constant.61.clone.gain.refs_17_) | copy-start | bytes 6291460
  11.9 10.9 %copy-start.8 = (bf16[128,32]{1,0:T(8,128)(2,1)S(1)}, bf16[128,32]{1,0:T(8,128)(2,1)}, u32[]{:S(2)}) copy-start(bf16[128,32]{1,0:T(8,128)(2,1)} %constant.63.clone.inject.refs_18_) | copy-start | bytes 24580
  11.9 10.9 %copy-start.11 = (f32[16,128]{1,0:T(8,128)S(1)}, f32[16,128]{1,0:T(8,128)}, u32[]{:S(2)}) copy-start(f32[16,128]{1,0:T(8,128)} %constant.70.clone.ends.refs_19_) | copy-start | bytes 24580
  15.7 6.6 %collective-permute-start.6 = (f32[96,128]{1,0:T(8,128)S(1)}, f32[96,128]{1,0:T(8,128)S(1)}, u32[]{:S(2)}, u32[]{:S(2)}) collective-permute-start(f32[96,128]{1,0:T(8,128)S(1)} %get-tuple-element.46), channel_id=1, source_target_pairs={{0,8},{1,4},{2,5},{3,6},{4,1},{5,2},{6,3},{7,15},{8,0},{9,12},{10,... | collective-permute-start | bytes 147464 | tf_op jit(solution)/shard_map/ppermute | solution.py:753
  17.6 6.9 %collective-permute-start.7 = (f32[96,128]{1,0:T(8,128)S(1)}, f32[96,128]{1,0:T(8,128)S(1)}, u32[]{:S(2)}, u32[]{:S(2)}) collective-permute-start(f32[96,128]{1,0:T(8,128)S(1)} %get-tuple-element.47), channel_id=1, source_target_pairs={{0,1},{1,0},{2,3},{3,2},{4,9},{5,10},{6,11},{7,15},{8,16},{9,4},{1... | collective-permute-start | bytes 147464 | tf_op jit(solution)/shard_map/ppermute | solution.py:753
  17.6 6.9 %collective-permute-start.8 = (f32[96,128]{1,0:T(8,128)S(1)}, f32[96,128]{1,0:T(8,128)S(1)}, u32[]{:S(2)}, u32[]{:S(2)}) collective-permute-start(f32[96,128]{1,0:T(8,128)S(1)} %get-tuple-element.48), channel_id=1, source_target_pairs={{0,5},{1,6},{2,7},{3,11},{4,12},{5,0},{6,1},{7,2},{8,13},{9,14},{1... | collective-permute-start | bytes 147464 | tf_op jit(solution)/shard_map/ppermute | solution.py:753
  21.2 3.3 %collective-permute-start.9 = (f32[96,128]{1,0:T(8,128)S(1)}, f32[96,128]{1,0:T(8,128)S(1)}, u32[]{:S(2)}, u32[]{:S(2)}) collective-permute-start(f32[96,128]{1,0:T(8,128)S(1)} %get-tuple-element.49), channel_id=1, source_target_pairs={{0,4},{1,2},{2,1},{3,11},{4,0},{5,8},{6,9},{7,10},{8,5},{9,6},{10,... | collective-permute-start | bytes 147464 | tf_op jit(solution)/shard_map/ppermute | solution.py:753
  21.2 4.6 %collective-permute-start.10 = (f32[96,128]{1,0:T(8,128)S(1)}, f32[96,128]{1,0:T(8,128)S(1)}, u32[]{:S(2)}, u32[]{:S(2)}) collective-permute-start(f32[96,128]{1,0:T(8,128)S(1)} %get-tuple-element.50), channel_id=1, source_target_pairs={{0,1},{1,0},{2,3},{3,2},{4,8},{5,9},{6,10},{7,11},{8,4},{9,5},{10,... | collective-permute-start | bytes 147464 | tf_op jit(solution)/shard_map/ppermute | solution.py:753
  22.3 3.5 %collective-permute-start.11 = (f32[96,128]{1,0:T(8,128)S(1)}, f32[96,128]{1,0:T(8,128)S(1)}, u32[]{:S(2)}, u32[]{:S(2)}) collective-permute-start(f32[96,128]{1,0:T(8,128)S(1)} %get-tuple-element.51), channel_id=1, source_target_pairs={{0,4},{1,5},{2,6},{3,7},{4,0},{5,1},{6,2},{7,3},{8,12},{9,13},{10,... | collective-permute-start | bytes 147464 | tf_op jit(solution)/shard_map/ppermute | solution.py:753
  27.0 5.2 %collective-permute-start.12 = (f32[96,128]{1,0:T(8,128)S(1)}, f32[96,128]{1,0:T(8,128)S(1)}, u32[]{:S(2)}, u32[]{:S(2)}) collective-permute-start(f32[96,128]{1,0:T(8,128)S(1)} %get-tuple-element.55), channel_id=1, source_target_pairs={{0,8},{1,4},{2,5},{3,6},{4,1},{5,2},{6,3},{7,15},{8,0},{9,12},{10,... | collective-permute-start | bytes 147464 | tf_op jit(solution)/shard_map/ppermute | solution.py:753
  28.6 5.5 %collective-permute-start.13 = (f32[96,128]{1,0:T(8,128)S(1)}, f32[96,128]{1,0:T(8,128)S(1)}, u32[]{:S(2)}, u32[]{:S(2)}) collective-permute-start(f32[96,128]{1,0:T(8,128)S(1)} %get-tuple-element.56), channel_id=1, source_target_pairs={{0,1},{1,0},{2,3},{3,2},{4,9},{5,10},{6,11},{7,15},{8,16},{9,4},{1... | collective-permute-start | bytes 147464 | tf_op jit(solution)/shard_map/ppermute | solution.py:753
  28.6 5.5 %collective-permute-start.14 = (f32[96,128]{1,0:T(8,128)S(1)}, f32[96,128]{1,0:T(8,128)S(1)}, u32[]{:S(2)}, u32[]{:S(2)}) collective-permute-start(f32[96,128]{1,0:T(8,128)S(1)} %get-tuple-element.57), channel_id=1, source_target_pairs={{0,5},{1,6},{2,7},{3,11},{4,12},{5,0},{6,1},{7,2},{8,13},{9,14},{1... | collective-permute-start | bytes 147464 | tf_op jit(solution)/shard_map/ppermute | solution.py:753
  30.8 3.3 %collective-permute-start.15 = (f32[96,128]{1,0:T(8,128)S(1)}, f32[96,128]{1,0:T(8,128)S(1)}, u32[]{:S(2)}, u32[]{:S(2)}) collective-permute-start(f32[96,128]{1,0:T(8,128)S(1)} %get-tuple-element.58), channel_id=1, source_target_pairs={{0,4},{1,2},{2,1},{3,11},{4,0},{5,8},{6,9},{7,10},{8,5},{9,6},{10,... | collective-permute-start | bytes 147464 | tf_op jit(solution)/shard_map/ppermute | solution.py:753
  30.8 4.3 %collective-permute-start.16 = (f32[96,128]{1,0:T(8,128)S(1)}, f32[96,128]{1,0:T(8,128)S(1)}, u32[]{:S(2)}, u32[]{:S(2)}) collective-permute-start(f32[96,128]{1,0:T(8,128)S(1)} %get-tuple-element.59), channel_id=1, source_target_pairs={{0,1},{1,0},{2,3},{3,2},{4,8},{5,9},{6,10},{7,11},{8,4},{9,5},{10,... | collective-permute-start | bytes 147464 | tf_op jit(solution)/shard_map/ppermute | solution.py:753
  32.2 2.8 %collective-permute-start.17 = (f32[96,128]{1,0:T(8,128)S(1)}, f32[96,128]{1,0:T(8,128)S(1)}, u32[]{:S(2)}, u32[]{:S(2)}) collective-permute-start(f32[96,128]{1,0:T(8,128)S(1)} %get-tuple-element.60), channel_id=1, source_target_pairs={{0,4},{1,5},{2,6},{3,7},{4,0},{5,1},{6,2},{7,3},{8,12},{9,13},{10,... | collective-permute-start | bytes 147464 | tf_op jit(solution)/shard_map/ppermute | solution.py:753
